TPU v7x, 32 devices: a whole 2x2x4 slice. The times are simulated.
32 devices in a mesh: section: 4 (over y, x), expert: 8 (over z, core).
Axes of the slice: x: 2, y: 2, z: 4, core: 2. Of those that a mesh axis runs over, the one named last changes fastest.
Arguments:
- tokens_in: bfloat16 [4, 256, 3584], P('section', 'expert'), may hold values from -6 to 6
- cotangent: bfloat16 [4, 256, 3584], P('section', 'expert'), may hold values from -6 to 6
- norm_gain: float32 [4, 3584], P('section'), may hold values from 0.1 to 1.9
- w_gate: bfloat16 [4, 8, 3584, 512], P('section', 'expert'), may hold values from -0.09375 to 0.09375
- w_up: bfloat16 [4, 8, 3584, 512], P('section', 'expert'), may hold values from -0.09375 to 0.09375
- w_down: bfloat16 [4, 8, 512, 3584], P('section', 'expert'), may hold values from -0.1875 to 0.1875
- expert_ids: int32 [4, 4, 256, 1], P('section', None, 'expert'), may hold values from 0 to 3; in each aligned block of 32 rows (0 to 31, 32 to 63, ..., all dimensions but the last counted through in order) at most 16 rows name the same one
- gate_weights: float32 [4, 4, 256, 1], P('section', None, 'expert'), may hold values from 0.2 to 1
Outputs:
- grad_inputs: bfloat16 [4, 4, 256, 3584], P('section', None, 'expert')
- grad_gates: float32 [4, 4, 256, 1], P('section', None, 'expert')
Inputs may be any that keep to these rules, and one draw needn't show every extreme that they name: `expert_ids`: within each aligned block of 32 tokens of one layer and micro-batch no expert is named more than 16 times, a bound that some block reaches; each token names one expert.
All inputs are finite; a program needn't handle non-finite values.
Results may differ from a plain program's by a relative error of at most 0.025.
Values may be sent and summed in bfloat16 or wider, within the bound.
No kernel may reach another device: no remote copies, remote signals or barrier semaphores. Data moves between devices by JAX's collectives and lax.ppermute only.
A program may use at most 192 MiB of HBM per device.

v0:
```python
from functools import partial

import jax
import jax.numpy as jnp
from jax import lax
from jax.sharding import PartitionSpec as P

epsilon = 1e-06


def shifted(block, axis, distance):
    devices = range(lax.axis_size(axis))
    route = [(i - distance, i) for i in devices if i - distance in devices]
    return lax.ppermute(block, axis, route)


def table_for(route_ids, expert_count, capacity):
    flat_ids = route_ids.reshape(-1)
    one_hot = (flat_ids[:, None] == jnp.arange(expert_count, dtype=jnp.int32)[None, :]).astype(
        jnp.int32
    )
    position = jnp.sum(
        (jnp.cumsum(one_hot, axis=0, dtype=jnp.int32) - 1) * one_hot, axis=-1, dtype=jnp.int32
    )
    slot_index = flat_ids * capacity + position
    place_table = (
        jnp.arange(expert_count * capacity, dtype=jnp.int32)[:, None] == slot_index[None, :]
    ).astype(jnp.bfloat16)
    return (slot_index, place_table)


def pick_entry(stored, chosen):
    return lax.dynamic_index_in_dim(stored, chosen, 0, keepdims=False)


def put_entry(stored, value, chosen, active):
    former = lax.dynamic_index_in_dim(stored, chosen, 0, keepdims=False)
    return lax.dynamic_update_index_in_dim(stored, jnp.where(active, value, former), chosen, 0)


def body(tokens_in, cotangent, norm_gain, w_gate, w_up, w_down, expert_ids, gate_weights):
    section_count = lax.axis_size("section")
    section_index = lax.axis_index("section")
    device_count = lax.axis_size("expert")
    expert_count = device_count // 2
    micro_count = expert_ids.shape[1]
    tok_rows = expert_ids.shape[2]
    picked = expert_ids.shape[3]
    model_dim = tokens_in.shape[2]
    capacity = 2 * ((tok_rows * picked + expert_count - 1) // expert_count)
    slot_rows = device_count * capacity
    inputs_all, cotangents_all = (
        lax.all_gather(tokens_in, "section", axis=0, tiled=True),
        lax.all_gather(cotangent, "section", axis=0, tiled=True),
    )
    gain_row = norm_gain[0]
    gate_mat = w_gate[0, 0]
    up_mat = w_up[0, 0]
    down_mat = w_down[0, 0]
    hidden_dim = gate_mat.shape[1]
    slot_all, place_all = jax.vmap(
        partial(table_for, expert_count=expert_count, capacity=capacity)
    )(expert_ids[0])
    route_weights = gate_weights[0]

    def dispatch(row_block, place_table):
        packed = jnp.dot(place_table, row_block, preferred_element_type=jnp.float32).astype(
            jnp.bfloat16
        )
        flat_rows = packed.reshape(expert_count, capacity * model_dim)
        doubled = jnp.concatenate([flat_rows, flat_rows], axis=1).reshape(
            device_count, capacity * model_dim
        )
        arrived = lax.all_to_all(doubled, "expert", split_axis=0, concat_axis=0, tiled=True)
        return arrived.reshape(slot_rows, model_dim)

    def collect(partial_out, slot_index):
        flat_rows = partial_out.reshape(device_count, capacity * model_dim)
        returned = lax.all_to_all(flat_rows, "expert", split_axis=0, concat_axis=0, tiled=True)
        paired = returned.reshape(expert_count, 2 * capacity * model_dim).astype(jnp.float32)
        span = capacity * model_dim
        summed = (paired[:, :span] + paired[:, span:]).reshape(expert_count * capacity, model_dim)
        return jnp.take(summed, slot_index, axis=0)

    def forward_expert(row_block):
        gate_pre = jnp.dot(row_block, gate_mat, preferred_element_type=jnp.float32)
        up_pre = jnp.dot(row_block, up_mat, preferred_element_type=jnp.float32)
        hidden = (jax.nn.silu(gate_pre) * up_pre).astype(jnp.bfloat16)
        return (
            jnp.dot(hidden, down_mat, preferred_element_type=jnp.float32).astype(jnp.bfloat16),
            gate_pre,
            up_pre,
        )

    def spare_forward(row_block):
        empty = jnp.zeros((slot_rows, hidden_dim), jnp.float32)
        return (jnp.zeros((slot_rows, model_dim), jnp.bfloat16), empty, empty)

    def backward_expert(operands):
        grad_block, gate_pre, up_pre = operands
        sigma = jax.nn.sigmoid(gate_pre)
        grad_hidden = jnp.dot(grad_block, down_mat.T, preferred_element_type=jnp.float32)
        grad_gate = (grad_hidden * up_pre * sigma * (1.0 + gate_pre * (1.0 - sigma))).astype(
            jnp.bfloat16
        )
        grad_up = (grad_hidden * gate_pre * sigma).astype(jnp.bfloat16)
        total = jnp.dot(grad_gate, gate_mat.T, preferred_element_type=jnp.float32)
        total = total + jnp.dot(grad_up, up_mat.T, preferred_element_type=jnp.float32)
        return total.astype(jnp.bfloat16)

    def spare_backward(operands):
        return jnp.zeros((slot_rows, model_dim), jnp.bfloat16)

    store_in = jnp.zeros((micro_count, tok_rows, model_dim), jnp.bfloat16)
    store_gate = jnp.zeros((micro_count, slot_rows, hidden_dim), jnp.float32)
    store_up = jnp.zeros((micro_count, slot_rows, hidden_dim), jnp.float32)
    store_rows = jnp.zeros((micro_count, tok_rows, picked * model_dim), jnp.float32)
    previous = jnp.zeros((tok_rows, model_dim), jnp.bfloat16)
    for moment in range(micro_count + section_count - 1):
        micro_index = moment - section_index
        active = (micro_index >= 0) & (micro_index < micro_count)
        chosen = jnp.clip(micro_index, 0, micro_count - 1)
        if moment == 0:
            received = previous
        else:
            received = shifted(previous, "section", 1)
        layer_in = jnp.where(section_index == 0, pick_entry(inputs_all, chosen), received)
        values = layer_in.astype(jnp.float32)
        inv_rms = lax.rsqrt(jnp.mean(values * values, axis=-1, keepdims=True) + epsilon)
        normed = (values * inv_rms * gain_row).astype(jnp.bfloat16)
        slot_index = pick_entry(slot_all, chosen)
        arrived = dispatch(jnp.repeat(normed, picked, axis=0), pick_entry(place_all, chosen))
        expert_out, gate_pre, up_pre = lax.cond(active, forward_expert, spare_forward, arrived)
        expert_rows = collect(expert_out, slot_index)
        weights_now = pick_entry(route_weights, chosen)
        mixed = values
        mixed = mixed + weights_now * expert_rows
        previous = mixed.astype(jnp.bfloat16)
        store_in = put_entry(store_in, layer_in, chosen, active)
        store_gate = put_entry(store_gate, gate_pre, chosen, active)
        store_up = put_entry(store_up, up_pre, chosen, active)
        store_rows = put_entry(store_rows, expert_rows, chosen, active)
    grad_out = jnp.zeros((micro_count, tok_rows, model_dim), jnp.bfloat16)
    gate_out = jnp.zeros((micro_count, tok_rows, picked), jnp.float32)
    previous = jnp.zeros((tok_rows, model_dim), jnp.bfloat16)
    for moment in range(micro_count + section_count - 1):
        micro_index = moment - (section_count - 1 - section_index)
        active = (micro_index >= 0) & (micro_index < micro_count)
        chosen = jnp.clip(micro_index, 0, micro_count - 1)
        if moment == 0:
            received = previous
        else:
            received = shifted(previous, "section", -1)
        grad_next = jnp.where(
            section_index == section_count - 1, pick_entry(cotangents_all, chosen), received
        )
        grad_f = grad_next.astype(jnp.float32)
        expert_rows = pick_entry(store_rows, chosen)
        weights_now = pick_entry(route_weights, chosen)
        gate_cols = [jnp.sum(grad_f * expert_rows, axis=-1)]
        grad_cols = weights_now * grad_f
        gate_grad = jnp.stack(gate_cols, axis=1)
        grad_rows = grad_cols.astype(jnp.bfloat16)
        slot_index = pick_entry(slot_all, chosen)
        arrived = dispatch(grad_rows, pick_entry(place_all, chosen))
        grad_part = lax.cond(
            active,
            backward_expert,
            spare_backward,
            (arrived, pick_entry(store_gate, chosen), pick_entry(store_up, chosen)),
        )
        collected = collect(grad_part, slot_index)
        scaled = collected * gain_row
        values = pick_entry(store_in, chosen).astype(jnp.float32)
        inv_rms = lax.rsqrt(jnp.mean(values * values, axis=-1, keepdims=True) + epsilon)
        grad_in = (
            grad_f
            + inv_rms * scaled
            - values
            * (inv_rms * inv_rms * inv_rms)
            * jnp.mean(values * scaled, axis=-1, keepdims=True)
        )
        previous = grad_in.astype(jnp.bfloat16)
        grad_out = put_entry(grad_out, previous, chosen, active)
        gate_out = put_entry(gate_out, gate_grad, chosen, active)
    return (grad_out[None], gate_out[None])


def solution(mesh):
    return jax.shard_map(
        body,
        mesh=mesh,
        in_specs=(
            P("section", "expert", None),
            P("section", "expert", None),
            P("section", None),
            P("section", "expert", None, None),
            P("section", "expert", None, None),
            P("section", "expert", None, None),
            P("section", None, "expert", None),
            P("section", None, "expert", None),
        ),
        out_specs=(P("section", None, "expert", None), P("section", None, "expert", None)),
        check_vma=False,
    )
```

profile of v0, /device:TPU:0, one launch (start us, length us, event | category | flops | bytes accessed | tf_op | source)
XLA Modules:
  0.0 1854.0 jit_solution(11186571991240202124)
XLA Ops:
  3.1 14.9 all_gather.7
  38.7 23.9 %all-to-all-done = bf16[8,2,28672]{2,1,0:T(2,128)(2,1)} async-done(((bf16[8,2,28672]{2,1,0:T(2,128)(2,1)}), bf16[8,2,28672]{2,1,0:T(2,128)(2,1)}, u32[]{:S(2)}, u32[]{:S(2)}) %all-to-all-start) | async-done | bytes 917536 | tf_op jit(solution)/shard_map/all_to_all | solution.py:74
  66.8 16.0 conditional.14
  101.7 22.1 %all-to-all-done.1 = bf16[8,2,28672]{2,1,0:T(2,128)(2,1)S(1)} async-done(((bf16[8,2,28672]{2,1,0:T(2,128)(2,1)}), bf16[8,2,28672]{2,1,0:T(2,128)(2,1)S(1)}, u32[]{:S(2)}, u32[]{:S(2)}) %all-to-all-start.1) | async-done | bytes 917536 | tf_op jit(solution)/shard_map/all_to_all | solution.py:79
  170.9 23.7 %all-to-all-done.2 = bf16[8,2,28672]{2,1,0:T(2,128)(2,1)S(1)} async-done(((bf16[8,2,28672]{2,1,0:T(2,128)(2,1)}), bf16[8,2,28672]{2,1,0:T(2,128)(2,1)S(1)}, u32[]{:S(2)}, u32[]{:S(2)}) %all-to-all-start.2) | async-done | bytes 917536 | tf_op jit(solution)/shard_map/all_to_all | solution.py:74
  197.9 17.2 conditional.15
  230.4 23.7 %all-to-all-done.3 = bf16[8,2,28672]{2,1,0:T(2,128)(2,1)S(1)} async-done(((bf16[8,2,28672]{2,1,0:T(2,128)(2,1)}), bf16[8,2,28672]{2,1,0:T(2,128)(2,1)S(1)}, u32[]{:S(2)}, u32[]{:S(2)}) %all-to-all-start.3) | async-done | bytes 917536 | tf_op jit(solution)/shard_map/all_to_all | solution.py:79
  305.0 23.7 %all-to-all-done.4 = bf16[8,2,28672]{2,1,0:T(2,128)(2,1)S(1)} async-done(((bf16[8,2,28672]{2,1,0:T(2,128)(2,1)}), bf16[8,2,28672]{2,1,0:T(2,128)(2,1)S(1)}, u32[]{:S(2)}, u32[]{:S(2)}) %all-to-all-start.4) | async-done | bytes 917536 | tf_op jit(solution)/shard_map/all_to_all | solution.py:74
  332.0 17.2 conditional.16
  364.5 23.7 %all-to-all-done.5 = bf16[8,2,28672]{2,1,0:T(2,128)(2,1)S(1)} async-done(((bf16[8,2,28672]{2,1,0:T(2,128)(2,1)}), bf16[8,2,28672]{2,1,0:T(2,128)(2,1)S(1)}, u32[]{:S(2)}, u32[]{:S(2)}) %all-to-all-start.5) | async-done | bytes 917536 | tf_op jit(solution)/shard_map/all_to_all | solution.py:79
  439.4 23.7 %all-to-all-done.6 = bf16[8,2,28672]{2,1,0:T(2,128)(2,1)S(1)} async-done(((bf16[8,2,28672]{2,1,0:T(2,128)(2,1)}), bf16[8,2,28672]{2,1,0:T(2,128)(2,1)S(1)}, u32[]{:S(2)}, u32[]{:S(2)}) %all-to-all-start.6) | async-done | bytes 917536 | tf_op jit(solution)/shard_map/all_to_all | solution.py:74
  466.4 16.8 conditional.17
  498.8 23.7 %all-to-all-done.7 = bf16[8,2,28672]{2,1,0:T(2,128)(2,1)S(1)} async-done(((bf16[8,2,28672]{2,1,0:T(2,128)(2,1)}), bf16[8,2,28672]{2,1,0:T(2,128)(2,1)S(1)}, u32[]{:S(2)}, u32[]{:S(2)}) %all-to-all-start.7) | async-done | bytes 917536 | tf_op jit(solution)/shard_map/all_to_all | solution.py:79
  525.8 8.0 convert_reduce_fusion.10
  574.0 16.2 all_gather.6
  639.5 10.7 all-to-all-done.9
  679.0 14.9 collective-permute-start.4
  730.8 11.8 all-to-all-done.10
  746.0 8.1 conditional.19
  780.2 14.3 all-to-all-done.11
  851.6 17.6 all-to-all-done.13
  877.9 8.8 conditional.21
  901.7 23.7 %all-to-all-done.14 = bf16[8,2,28672]{2,1,0:T(2,128)(2,1)S(1)} async-done(((bf16[8,2,28672]{2,1,0:T(2,128)(2,1)}), bf16[8,2,28672]{2,1,0:T(2,128)(2,1)S(1)}, u32[]{:S(2)}, u32[]{:S(2)}) %all-to-all-start.14) | async-done | bytes 917536 | tf_op jit(solution)/shard_map/all_to_all | solution.py:79
  949.9 19.4 %collective-permute-done.6 = bf16[32,3584]{1,0:T(8,128)(2,1)S(1)} collective-permute-done((bf16[32,3584]{1,0:T(8,128)(2,1)S(1)}, bf16[32,3584]{1,0:T(8,128)(2,1)S(1)}, u32[]{:S(2)}, u32[]{:S(2)}) %collective-permute-start.6) | collective-permute-done | bytes 229408 | tf_op jit(solution)/shard_map/ppermute | solution.py:14
  979.4 8.5 reduce.58
  995.0 23.8 %all-to-all-done.15 = bf16[8,2,28672]{2,1,0:T(2,128)(2,1)} async-done(((bf16[8,2,28672]{2,1,0:T(2,128)(2,1)}), bf16[8,2,28672]{2,1,0:T(2,128)(2,1)}, u32[]{:S(2)}, u32[]{:S(2)}) %all-to-all-start.15) | async-done | bytes 917536 | tf_op jit(solution)/shard_map/all_to_all | solution.py:74
  1034.8 8.5 reduce.59
  1051.3 23.0 %all-to-all-done.16 = bf16[8,2,28672]{2,1,0:T(2,128)(2,1)} async-done(((bf16[8,2,28672]{2,1,0:T(2,128)(2,1)}), bf16[8,2,28672]{2,1,0:T(2,128)(2,1)}, u32[]{:S(2)}, u32[]{:S(2)}) %all-to-all-start.16) | async-done | bytes 917536 | tf_op jit(solution)/shard_map/all_to_all | solution.py:79
  1102.6 9.1 collective-permute-done.7
  1131.5 23.7 %all-to-all-done.17 = bf16[8,2,28672]{2,1,0:T(2,128)(2,1)S(1)} async-done(((bf16[8,2,28672]{2,1,0:T(2,128)(2,1)}), bf16[8,2,28672]{2,1,0:T(2,128)(2,1)S(1)}, u32[]{:S(2)}, u32[]{:S(2)}) %all-to-all-start.17) | async-done | bytes 917536 | tf_op jit(solution)/shard_map/all_to_all | solution.py:74
  1180.9 22.0 %all-to-all-done.18 = bf16[8,2,28672]{2,1,0:T(2,128)(2,1)S(1)} async-done(((bf16[8,2,28672]{2,1,0:T(2,128)(2,1)}), bf16[8,2,28672]{2,1,0:T(2,128)(2,1)S(1)}, u32[]{:S(2)}, u32[]{:S(2)}) %all-to-all-start.18) | async-done | bytes 917536 | tf_op jit(solution)/shard_map/all_to_all | solution.py:79
  1228.9 53.1 %collective-permute-done.8 = bf16[32,3584]{1,0:T(8,128)(2,1)S(1)} collective-permute-done((bf16[32,3584]{1,0:T(8,128)(2,1)S(1)}, bf16[32,3584]{1,0:T(8,128)(2,1)S(1)}, u32[]{:S(2)}, u32[]{:S(2)}) %collective-permute-start.8) | collective-permute-done | bytes 229408 | tf_op jit(solution)/shard_map/ppermute | solution.py:14
  1307.2 19.6 %all-to-all-done.19 = bf16[8,2,28672]{2,1,0:T(2,128)(2,1)} async-done(((bf16[8,2,28672]{2,1,0:T(2,128)(2,1)}), bf16[8,2,28672]{2,1,0:T(2,128)(2,1)}, u32[]{:S(2)}, u32[]{:S(2)}) %all-to-all-start.19) | async-done | bytes 917536 | tf_op jit(solution)/shard_map/all_to_all | solution.py:74
  1332.4 16.8 conditional.24
  1351.3 8.6 reduce.63
  1371.7 19.4 %all-to-all-done.20 = bf16[8,2,28672]{2,1,0:T(2,128)(2,1)} async-done(((bf16[8,2,28672]{2,1,0:T(2,128)(2,1)}), bf16[8,2,28672]{2,1,0:T(2,128)(2,1)}, u32[]{:S(2)}, u32[]{:S(2)}) %all-to-all-start.20) | async-done | bytes 917536 | tf_op jit(solution)/shard_map/all_to_all | solution.py:79
  1450.7 20.7 %all-to-all-done.21 = bf16[8,2,28672]{2,1,0:T(2,128)(2,1)S(1)} async-done(((bf16[8,2,28672]{2,1,0:T(2,128)(2,1)}), bf16[8,2,28672]{2,1,0:T(2,128)(2,1)S(1)}, u32[]{:S(2)}, u32[]{:S(2)}) %all-to-all-start.21) | async-done | bytes 917536 | tf_op jit(solution)/shard_map/all_to_all | solution.py:74
  1474.7 17.3 conditional.25
  1494.1 8.5 reduce.65
  1512.6 21.2 %all-to-all-done.22 = bf16[8,2,28672]{2,1,0:T(2,128)(2,1)} async-done(((bf16[8,2,28672]{2,1,0:T(2,128)(2,1)}), bf16[8,2,28672]{2,1,0:T(2,128)(2,1)}, u32[]{:S(2)}, u32[]{:S(2)}) %all-to-all-start.22) | async-done | bytes 917536 | tf_op jit(solution)/shard_map/all_to_all | solution.py:79
  1586.1 8.5 reduce.66
  1615.5 8.0 convert_reduce_fusion
  1636.6 17.1 conditional.26
  1677.3 16.2 all-to-all-done.24
  1720.8 8.2 collective-permute-done.11
  1748.6 23.7 %all-to-all-done.25 = bf16[8,2,28672]{2,1,0:T(2,128)(2,1)S(1)} async-done(((bf16[8,2,28672]{2,1,0:T(2,128)(2,1)}), bf16[8,2,28672]{2,1,0:T(2,128)(2,1)S(1)}, u32[]{:S(2)}, u32[]{:S(2)}) %all-to-all-start.25) | async-done | bytes 917536 | tf_op jit(solution)/shard_map/all_to_all | solution.py:74
  1775.6 17.1 conditional.27
  1809.0 22.3 %all-to-all-done.26 = bf16[8,2,28672]{2,1,0:T(2,128)(2,1)S(1)} async-done(((bf16[8,2,28672]{2,1,0:T(2,128)(2,1)}), bf16[8,2,28672]{2,1,0:T(2,128)(2,1)S(1)}, u32[]{:S(2)}, u32[]{:S(2)}) %all-to-all-start.26) | async-done | bytes 917536 | tf_op jit(solution)/shard_map/all_to_all | solution.py:79
  (628 shorter events, 1142.1 us)
Async XLA Ops:
  17.9 681.2 %copy-start.28 = (bf16[4,32,3584]{2,1,0:T(8,128)(2,1)}, bf16[4,32,3584]{2,1,0:T(8,128)(2,1)S(1)}, u32[]{:S(2)}) copy-start(bf16[4,32,3584]{2,1,0:T(8,128)(2,1)S(1)} %all_gather.7) | copy-start | bytes 2752516
  33.9 28.8 %all-to-all-start = ((bf16[8,2,28672]{2,1,0:T(2,128)(2,1)}), bf16[8,2,28672]{2,1,0:T(2,128)(2,1)}, u32[]{:S(2)}, u32[]{:S(2)}) async-start(bf16[8,2,28672]{2,1,0:T(2,128)(2,1)} %reshape.918), calls=%async_computation | async-start | bytes 1835008 | tf_op jit(solution)/shard_map/all_to_all | solution.py:74
  96.1 27.7 %all-to-all-start.1 = ((bf16[8,2,28672]{2,1,0:T(2,128)(2,1)}), bf16[8,2,28672]{2,1,0:T(2,128)(2,1)S(1)}, u32[]{:S(2)}, u32[]{:S(2)}) async-start(bf16[8,2,28672]{2,1,0:T(2,128)(2,1)} %reshape.920), calls=%async_computation.1 | async-start | bytes 1835008 | tf_op jit(solution)/shard_map/all_to_all | solution.py:79
  100.9 43.1 %copy-start.66 = (pred[32]{0:T(512)(128)(4,1)}, pred[32]{0:T(512)(128)(4,1)S(1)}, u32[]{:S(2)}) copy-start(pred[32]{0:T(512)(128)(4,1)S(1)} %get-tuple-element.838) | copy-start | bytes 100
  100.9 173.3 %copy-start.74 = (pred[32]{0:T(512)(128)(4,1)}, pred[32]{0:T(512)(128)(4,1)S(1)}, u32[]{:S(2)}) copy-start(pred[32]{0:T(512)(128)(4,1)S(1)} %get-tuple-element.836) | copy-start | bytes 100
  100.9 307.4 %copy-start.71 = (pred[32]{0:T(512)(128)(4,1)}, pred[32]{0:T(512)(128)(4,1)S(1)}, u32[]{:S(2)}) copy-start(pred[32]{0:T(512)(128)(4,1)S(1)} %get-tuple-element.834) | copy-start | bytes 100
  144.1 6.2 collective-permute-start
  167.3 27.3 %all-to-all-start.2 = ((bf16[8,2,28672]{2,1,0:T(2,128)(2,1)}), bf16[8,2,28672]{2,1,0:T(2,128)(2,1)S(1)}, u32[]{:S(2)}, u32[]{:S(2)}) async-start(bf16[8,2,28672]{2,1,0:T(2,128)(2,1)} %reshape.922), calls=%async_computation.2 | async-start | bytes 1835008 | tf_op jit(solution)/shard_map/all_to_all | solution.py:74
  226.3 27.7 %all-to-all-start.3 = ((bf16[8,2,28672]{2,1,0:T(2,128)(2,1)}), bf16[8,2,28672]{2,1,0:T(2,128)(2,1)S(1)}, u32[]{:S(2)}, u32[]{:S(2)}) async-start(bf16[8,2,28672]{2,1,0:T(2,128)(2,1)} %reshape.924), calls=%async_computation.3 | async-start | bytes 1835008 | tf_op jit(solution)/shard_map/all_to_all | solution.py:79
  275.5 9.0 collective-permute-start.1
  301.5 27.3 %all-to-all-start.4 = ((bf16[8,2,28672]{2,1,0:T(2,128)(2,1)}), bf16[8,2,28672]{2,1,0:T(2,128)(2,1)S(1)}, u32[]{:S(2)}, u32[]{:S(2)}) async-start(bf16[8,2,28672]{2,1,0:T(2,128)(2,1)} %reshape.926), calls=%async_computation.4 | async-start | bytes 1835008 | tf_op jit(solution)/shard_map/all_to_all | solution.py:74
  360.5 27.7 %all-to-all-start.5 = ((bf16[8,2,28672]{2,1,0:T(2,128)(2,1)}), bf16[8,2,28672]{2,1,0:T(2,128)(2,1)S(1)}, u32[]{:S(2)}, u32[]{:S(2)}) async-start(bf16[8,2,28672]{2,1,0:T(2,128)(2,1)} %reshape.928), calls=%async_computation.5 | async-start | bytes 1835008 | tf_op jit(solution)/shard_map/all_to_all | solution.py:79
  409.6 9.0 collective-permute-start.2
  435.6 27.5 %all-to-all-start.6 = ((bf16[8,2,28672]{2,1,0:T(2,128)(2,1)}), bf16[8,2,28672]{2,1,0:T(2,128)(2,1)S(1)}, u32[]{:S(2)}, u32[]{:S(2)}) async-start(bf16[8,2,28672]{2,1,0:T(2,128)(2,1)} %reshape.930), calls=%async_computation.6 | async-start | bytes 1835008 | tf_op jit(solution)/shard_map/all_to_all | solution.py:74
  494.7 27.7 %all-to-all-start.7 = ((bf16[8,2,28672]{2,1,0:T(2,128)(2,1)}), bf16[8,2,28672]{2,1,0:T(2,128)(2,1)S(1)}, u32[]{:S(2)}, u32[]{:S(2)}) async-start(bf16[8,2,28672]{2,1,0:T(2,128)(2,1)} %reshape.932), calls=%async_computation.7 | async-start | bytes 1835008 | tf_op jit(solution)/shard_map/all_to_all | solution.py:79
  543.7 9.0 collective-permute-start.3
  569.7 28.0 %all-to-all-start.8 = ((bf16[8,2,28672]{2,1,0:T(2,128)(2,1)}), bf16[8,2,28672]{2,1,0:T(2,128)(2,1)}, u32[]{:S(2)}, u32[]{:S(2)}) async-start(bf16[8,2,28672]{2,1,0:T(2,128)(2,1)} %reshape.934), calls=%async_computation.8 | async-start | bytes 1835008 | tf_op jit(solution)/shard_map/all_to_all | solution.py:74
  621.6 28.5 %all-to-all-start.9 = ((bf16[8,2,28672]{2,1,0:T(2,128)(2,1)}), bf16[8,2,28672]{2,1,0:T(2,128)(2,1)}, u32[]{:S(2)}, u32[]{:S(2)}) async-start(bf16[8,2,28672]{2,1,0:T(2,128)(2,1)} %reshape.936), calls=%async_computation.9 | async-start | bytes 1835008 | tf_op jit(solution)/shard_map/all_to_all | solution.py:79
  650.1 64.0 %all-to-all-start.12 = ((bf16[8,2,28672]{2,1,0:T(2,128)(2,1)}), bf16[8,2,28672]{2,1,0:T(2,128)(2,1)}, u32[]{:S(2)}, u32[]{:S(2)}) async-start(bf16[8,2,28672]{2,1,0:T(2,128)(2,1)} %reshape.916), calls=%async_computation.12 | async-start | bytes 1835008 | tf_op jit(solution)/shard_map/all_to_all | solution.py:74
  679.0 20.1 %collective-permute-start.4 = (bf16[32,3584]{1,0:T(8,128)(2,1)S(1)}, bf16[32,3584]{1,0:T(8,128)(2,1)S(1)}, u32[]{:S(2)}, u32[]{:S(2)}) collective-permute-start(bf16[32,3584]{1,0:T(8,128)(2,1)S(1)} %fusion.177), channel_id=1, source_target_pairs={{0,8},{8,16},{16,24},{1,9},{9,17},{17,25},{2,10},{10,18},{18,26},{... | collective-permute-start | bytes 688136 | tf_op jit(solution)/shard_map/ppermute | solution.py:14
  714.1 28.6 %all-to-all-start.10 = ((bf16[8,2,28672]{2,1,0:T(2,128)(2,1)}), bf16[8,2,28672]{2,1,0:T(2,128)(2,1)S(1)}, u32[]{:S(2)}, u32[]{:S(2)}) async-start(bf16[8,2,28672]{2,1,0:T(2,128)(2,1)} %reshape.938), calls=%async_computation.10 | async-start | bytes 1835008 | tf_op jit(solution)/shard_map/all_to_all | solution.py:74
  767.0 27.4 %all-to-all-start.11 = ((bf16[8,2,28672]{2,1,0:T(2,128)(2,1)}), bf16[8,2,28672]{2,1,0:T(2,128)(2,1)S(1)}, u32[]{:S(2)}, u32[]{:S(2)}) async-start(bf16[8,2,28672]{2,1,0:T(2,128)(2,1)} %reshape.940), calls=%async_computation.11 | async-start | bytes 1835008 | tf_op jit(solution)/shard_map/all_to_all | solution.py:79
  816.6 9.5 collective-permute-start.5
  841.9 27.3 %all-to-all-start.13 = ((bf16[8,2,28672]{2,1,0:T(2,128)(2,1)}), bf16[8,2,28672]{2,1,0:T(2,128)(2,1)S(1)}, u32[]{:S(2)}, u32[]{:S(2)}) async-start(bf16[8,2,28672]{2,1,0:T(2,128)(2,1)} %reshape.942), calls=%async_computation.13 | async-start | bytes 1835008 | tf_op jit(solution)/shard_map/all_to_all | solution.py:74
  897.9 27.5 %all-to-all-start.14 = ((bf16[8,2,28672]{2,1,0:T(2,128)(2,1)}), bf16[8,2,28672]{2,1,0:T(2,128)(2,1)S(1)}, u32[]{:S(2)}, u32[]{:S(2)}) async-start(bf16[8,2,28672]{2,1,0:T(2,128)(2,1)} %reshape.944), calls=%async_computation.14 | async-start | bytes 1835008 | tf_op jit(solution)/shard_map/all_to_all | solution.py:79
  948.4 102.2 %copy-start.29 = (bf16[4,32,3584]{2,1,0:T(8,128)(2,1)}, bf16[4,32,3584]{2,1,0:T(8,128)(2,1)S(1)}, u32[]{:S(2)}) copy-start(bf16[4,32,3584]{2,1,0:T(8,128)(2,1)S(1)} %get-tuple-element.786) | copy-start | bytes 2752516
  948.4 21.0 %collective-permute-start.6 = (bf16[32,3584]{1,0:T(8,128)(2,1)S(1)}, bf16[32,3584]{1,0:T(8,128)(2,1)S(1)}, u32[]{:S(2)}, u32[]{:S(2)}) collective-permute-start(bf16[32,3584]{1,0:T(8,128)(2,1)S(1)} %get-tuple-element.787), channel_id=1, source_target_pairs={{8,0},{16,8},{24,16},{9,1},{17,9},{25,17},{10,2},{18,10},{26,18},{... | collective-permute-start | bytes 688136 | tf_op jit(solution)/shard_map/ppermute | solution.py:14
  990.8 28.0 %all-to-all-start.15 = ((bf16[8,2,28672]{2,1,0:T(2,128)(2,1)}), bf16[8,2,28672]{2,1,0:T(2,128)(2,1)}, u32[]{:S(2)}, u32[]{:S(2)}) async-start(bf16[8,2,28672]{2,1,0:T(2,128)(2,1)} %reshape.946), calls=%async_computation.15 | async-start | bytes 1835008 | tf_op jit(solution)/shard_map/all_to_all | solution.py:74
  1046.1 28.2 %all-to-all-start.16 = ((bf16[8,2,28672]{2,1,0:T(2,128)(2,1)}), bf16[8,2,28672]{2,1,0:T(2,128)(2,1)}, u32[]{:S(2)}, u32[]{:S(2)}) async-start(bf16[8,2,28672]{2,1,0:T(2,128)(2,1)} %reshape.948), calls=%async_computation.16 | async-start | bytes 1835008 | tf_op jit(solution)/shard_map/all_to_all | solution.py:79
  1097.6 15.8 copy-start.89
  1101.0 10.7 collective-permute-start.7
  1128.0 27.3 %all-to-all-start.17 = ((bf16[8,2,28672]{2,1,0:T(2,128)(2,1)}), bf16[8,2,28672]{2,1,0:T(2,128)(2,1)S(1)}, u32[]{:S(2)}, u32[]{:S(2)}) async-start(bf16[8,2,28672]{2,1,0:T(2,128)(2,1)} %reshape.950), calls=%async_computation.17 | async-start | bytes 1835008 | tf_op jit(solution)/shard_map/all_to_all | solution.py:74
  1175.5 27.5 %all-to-all-start.18 = ((bf16[8,2,28672]{2,1,0:T(2,128)(2,1)}), bf16[8,2,28672]{2,1,0:T(2,128)(2,1)S(1)}, u32[]{:S(2)}, u32[]{:S(2)}) async-start(bf16[8,2,28672]{2,1,0:T(2,128)(2,1)} %reshape.952), calls=%async_computation.18 | async-start | bytes 1835008 | tf_op jit(solution)/shard_map/all_to_all | solution.py:79
  1223.8 59.7 %copy-start.88 = (f32[32]{0:T(128)S(1)}, f32[32]{0:T(128)}, u32[]{:S(2)}) copy-start(f32[32]{0:T(128)} %get-tuple-element.842) | copy-start | bytes 388
  1227.3 54.7 %collective-permute-start.8 = (bf16[32,3584]{1,0:T(8,128)(2,1)S(1)}, bf16[32,3584]{1,0:T(8,128)(2,1)S(1)}, u32[]{:S(2)}, u32[]{:S(2)}) collective-permute-start(bf16[32,3584]{1,0:T(8,128)(2,1)S(1)} %get-tuple-element.779), channel_id=1, source_target_pairs={{8,0},{16,8},{24,16},{9,1},{17,9},{25,17},{10,2},{18,10},{26,18},{... | collective-permute-start | bytes 688136 | tf_op jit(solution)/shard_map/ppermute | solution.py:14
  1298.1 28.6 %all-to-all-start.19 = ((bf16[8,2,28672]{2,1,0:T(2,128)(2,1)}), bf16[8,2,28672]{2,1,0:T(2,128)(2,1)}, u32[]{:S(2)}, u32[]{:S(2)}) async-start(bf16[8,2,28672]{2,1,0:T(2,128)(2,1)} %reshape.954), calls=%async_computation.19 | async-start | bytes 1835008 | tf_op jit(solution)/shard_map/all_to_all | solution.py:74
  1362.9 28.2 %all-to-all-start.20 = ((bf16[8,2,28672]{2,1,0:T(2,128)(2,1)}), bf16[8,2,28672]{2,1,0:T(2,128)(2,1)}, u32[]{:S(2)}, u32[]{:S(2)}) async-start(bf16[8,2,28672]{2,1,0:T(2,128)(2,1)} %reshape.956), calls=%async_computation.20 | async-start | bytes 1835008 | tf_op jit(solution)/shard_map/all_to_all | solution.py:79
  1417.9 9.9 collective-permute-start.9
  1444.1 27.3 %all-to-all-start.21 = ((bf16[8,2,28672]{2,1,0:T(2,128)(2,1)}), bf16[8,2,28672]{2,1,0:T(2,128)(2,1)S(1)}, u32[]{:S(2)}, u32[]{:S(2)}) async-start(bf16[8,2,28672]{2,1,0:T(2,128)(2,1)} %reshape.958), calls=%async_computation.21 | async-start | bytes 1835008 | tf_op jit(solution)/shard_map/all_to_all | solution.py:74
  1505.6 28.2 %all-to-all-start.22 = ((bf16[8,2,28672]{2,1,0:T(2,128)(2,1)}), bf16[8,2,28672]{2,1,0:T(2,128)(2,1)}, u32[]{:S(2)}, u32[]{:S(2)}) async-start(bf16[8,2,28672]{2,1,0:T(2,128)(2,1)} %reshape.960), calls=%async_computation.22 | async-start | bytes 1835008 | tf_op jit(solution)/shard_map/all_to_all | solution.py:79
  1558.6 20.4 %collective-permute-start.10 = (bf16[32,3584]{1,0:T(8,128)(2,1)}, bf16[32,3584]{1,0:T(8,128)(2,1)}, u32[]{:S(2)}, u32[]{:S(2)}) collective-permute-start(bf16[32,3584]{1,0:T(8,128)(2,1)} %get-tuple-element.771), channel_id=1, source_target_pairs={{8,0},{16,8},{24,16},{9,1},{17,9},{25,17},{10,2},{18,10},{26,18},{... | collective-permute-start | bytes 688136 | tf_op jit(solution)/shard_map/ppermute | solution.py:14
  1574.3 28.5 %all-to-all-start.27 = ((bf16[8,2,28672]{2,1,0:T(2,128)(2,1)}), bf16[8,2,28672]{2,1,0:T(2,128)(2,1)}, u32[]{:S(2)}, u32[]{:S(2)}) async-start(bf16[8,2,28672]{2,1,0:T(2,128)(2,1)} %reshape.970), calls=%async_computation.27 | async-start | bytes 1835008 | tf_op jit(solution)/shard_map/all_to_all | solution.py:79
  1602.8 28.2 %all-to-all-start.23 = ((bf16[8,2,28672]{2,1,0:T(2,128)(2,1)}), bf16[8,2,28672]{2,1,0:T(2,128)(2,1)}, u32[]{:S(2)}, u32[]{:S(2)}) async-start(bf16[8,2,28672]{2,1,0:T(2,128)(2,1)} %reshape.962), calls=%async_computation.23 | async-start | bytes 1835008 | tf_op jit(solution)/shard_map/all_to_all | solution.py:74
  1665.0 28.5 %all-to-all-start.24 = ((bf16[8,2,28672]{2,1,0:T(2,128)(2,1)}), bf16[8,2,28672]{2,1,0:T(2,128)(2,1)}, u32[]{:S(2)}, u32[]{:S(2)}) async-start(bf16[8,2,28672]{2,1,0:T(2,128)(2,1)} %reshape.964), calls=%async_computation.24 | async-start | bytes 1835008 | tf_op jit(solution)/shard_map/all_to_all | solution.py:79
  1718.5 10.6 collective-permute-start.11
  1745.0 27.3 %all-to-all-start.25 = ((bf16[8,2,28672]{2,1,0:T(2,128)(2,1)}), bf16[8,2,28672]{2,1,0:T(2,128)(2,1)S(1)}, u32[]{:S(2)}, u32[]{:S(2)}) async-start(bf16[8,2,28672]{2,1,0:T(2,128)(2,1)} %reshape.966), calls=%async_computation.25 | async-start | bytes 1835008 | tf_op jit(solution)/shard_map/all_to_all | solution.py:74
  1804.0 27.3 %all-to-all-start.26 = ((bf16[8,2,28672]{2,1,0:T(2,128)(2,1)}), bf16[8,2,28672]{2,1,0:T(2,128)(2,1)S(1)}, u32[]{:S(2)}, u32[]{:S(2)}) async-start(bf16[8,2,28672]{2,1,0:T(2,128)(2,1)} %reshape.968), calls=%async_computation.26 | async-start | bytes 1835008 | tf_op jit(solution)/shard_map/all_to_all | solution.py:79
  1808.9 33.6 %copy-start.65 = (f32[1,4,32,1]{2,1,3,0:T(4,128)}, f32[1,4,32,1]{2,1,3,0:T(4,128)S(1)}, u32[]{:S(2)}) copy-start(f32[1,4,32,1]{2,1,3,0:T(4,128)S(1)} %dynamic_update_slice.173) | copy-start | bytes 1540
  (70 other events, 370.9 us)
where the time goes:
time: 1870 us; the launch traced here: 1850 us
  waiting for transfers between devices  640 us (34%)
  other arithmetic  511 us (27%)
  local copies, waits for them, and re-layouts  414 us (22%)
  starting transfers between devices  159 us (9%)
  matrix products  61.5 us (3%)
  loops' own time  34.5 us (2%)
  blocking collectives  31 us (2%)
    all_to_all x14, waiting for transfers between devices, collect(): lax.all_to_all(flat_rows, 'expert', split_axis=0, concat_axis=0, tiled=True)  271 us
    all_to_all x14, waiting for transfers between devices, dispatch(): lax.all_to_all(doubled, 'expert', split_axis=0, concat_axis=0, tiled=True)  244 us
    unnamed x181, local copies, waits for them, and re-layouts  182 us
    ppermute x12, waiting for transfers between devices, shifted(): return lax.ppermute(block, axis, route)  125 us
    convert_element_type x14, other arithmetic, collect(): returned.reshape(expert_count, 2 * capacity * model_dim).astype(jnp.float32)  111 us
    all_to_all x14, other arithmetic, collect(): lax.all_to_all(flat_rows, 'expert', split_axis=0, concat_axis=0, tiled=True)  108 us
    all_to_all x14, other arithmetic, dispatch(): lax.all_to_all(doubled, 'expert', split_axis=0, concat_axis=0, tiled=True)  107 us
    another operation x8, other arithmetic  61.2 us
  transfers between devices with their start and end apart: 40, of which 38 were waited for; matrix products, arithmetic and copies ran while one was open for 8% of the time, Pallas kernels for 0%

commit v1 on v0

v1 whole, which is shorter than its diff:
```python
from functools import partial

import jax
import jax.numpy as jnp
from jax import lax
from jax.experimental import pallas as pl
from jax.experimental.pallas import tpu as pltpu
from jax.sharding import PartitionSpec as P

epsilon = 1e-06
both = ("section", "expert")
last_with_last = (((1,), (1,)), ((), ()))

in_vmem = pl.BlockSpec(memory_space=pltpu.VMEM)
in_smem = pl.BlockSpec(memory_space=pltpu.SMEM)
anywhere = pl.BlockSpec(memory_space=pl.ANY)


def spans(total, size):
    size = size if total % size == 0 else total
    return [pl.ds(start, size) for start in range(0, total, size)]


def params(mib):
    return pltpu.CompilerParams(vmem_limit_bytes=mib * 2**20)


def product(left, right):
    return jnp.dot(left, right, preferred_element_type=jnp.float32)


def product_t(left, right):
    return lax.dot_general(left, right, last_with_last, preferred_element_type=jnp.float32)


def weight_copies(half_refs, buffers, sems):
    return [
        [
            pltpu.make_async_copy(half_refs[half][which], buffers[which].at[half], sems.at[which, half])
            for half in range(2)
        ]
        for which in range(3)
    ]


def forward_kernel(slot, micro_count, parts, *refs):
    sec_ref, gain_ref, route_ref = refs[:3]
    x_refs = refs[3 : 3 + parts]
    rest = refs[3 + parts :]
    half_refs = [rest[0:3], rest[3:6]]
    out_refs = rest[6 : 6 + parts]
    save_x, save_gate, save_up, save_rows = rest[6 + parts : 10 + parts]
    gate_buf, up_buf, down_buf, normed, hidden, sems = rest[10 + parts :]
    micro = slot - sec_ref[0]
    width = gain_ref.shape[1]
    hidden_dim = gate_buf.shape[2]
    rows = x_refs[0].shape[0]

    @pl.when((micro >= 0) & (micro < micro_count))
    def _():
        copies = weight_copies(half_refs, (gate_buf, up_buf, down_buf), sems)
        for half in range(2):
            copies[0][half].start()
            copies[1][half].start()
        for half in range(2):
            copies[2][half].start()
        for part in range(parts):
            block = x_refs[part][...]
            values = block.astype(jnp.float32)
            inv_rms = lax.rsqrt(jnp.mean(values * values, axis=-1, keepdims=True) + epsilon)
            here = pl.ds(part * rows, rows)
            normed[here, :] = (values * inv_rms * gain_ref[...]).astype(jnp.bfloat16)
            save_x[here, :] = block
        for half in range(2):
            side = pl.ds(half * hidden_dim, hidden_dim)
            copies[0][half].wait()
            gate_pre = product(normed[...], gate_buf[half])
            copies[1][half].wait()
            up_pre = product(normed[...], up_buf[half])
            save_gate[:, side] = gate_pre
            save_up[:, side] = up_pre
            hidden[half] = (gate_pre * jax.nn.sigmoid(gate_pre) * up_pre).astype(jnp.bfloat16)
        copies[2][0].wait()
        copies[2][1].wait()
        route = route_ref[micro]
        for span in spans(width, 256):
            made = product(hidden[0], down_buf[0, :, span])
            made = made + product(hidden[1], down_buf[1, :, span])
            save_rows[:, span] = made
            added = route * made
            for part in range(parts):
                here = slice(part * rows, (part + 1) * rows)
                values = x_refs[part][:, span].astype(jnp.float32)
                out_refs[part][:, span] = (values + added[here]).astype(jnp.bfloat16)


def backward_kernel(slot, counts, candidates, parts, *refs):
    section_count, micro_count = counts
    sec_ref, gain_ref, route_ref = refs[:3]
    rest = refs[3:]
    arrived = rest[:parts]
    first = rest[parts : 2 * parts]
    rest = rest[2 * parts :]
    half_refs = [rest[0:3], rest[3:6]]
    rest = rest[6:]
    saved = {}
    for section in candidates:
        saved[section] = rest[:4]
        rest = rest[4:]
    out_refs = rest[:parts]
    gate_out = rest[parts]
    (gate_buf, up_buf, down_buf, grad_buf, x_buf, pre_gate, pre_up, rows_buf, grad_rows, scaled_buf,
     sems, state_sems, grad_sems) = rest[parts + 1 :]
    sec = sec_ref[0]
    micro = slot - 2 * (section_count - 1) + sec
    width = gain_ref.shape[1]
    hidden_dim = gate_buf.shape[2]
    slots = grad_buf.shape[0]
    rows = slots // parts

    @pl.when((micro >= 0) & (micro < micro_count))
    def _():
        def for_section(section, act):
            @pl.when(sec == section)
            def _():
                for part in range(parts):
                    if section == section_count - 1:
                        source = first[part].at[slot - (section_count - 1)]
                    else:
                        source = arrived[part]
                    act(pltpu.make_async_copy(
                        source, grad_buf.at[pl.ds(part * rows, rows), :], grad_sems.at[part]
                    ))
                targets = (rows_buf, x_buf, pre_gate, pre_up)
                for number, target in enumerate(targets):
                    act(pltpu.make_async_copy(
                        saved[section][number], target, state_sems.at[number]
                    ))

        for section in candidates:
            for_section(section, lambda copy: copy.start())
        copies = weight_copies(half_refs, (gate_buf, up_buf, down_buf), sems)
        for half in range(2):
            copies[2][half].start()
        for half in range(2):
            copies[0][half].start()
            copies[1][half].start()
        for section in candidates:
            for_section(section, lambda copy: copy.wait())
        route = route_ref[micro]
        gate_grad = jnp.zeros((slots, 1), jnp.float32)
        square = jnp.zeros((slots, 1), jnp.float32)
        for span in spans(width, 512):
            grad_f = grad_buf[:, span].astype(jnp.float32)
            gate_grad += jnp.sum(grad_f * rows_buf[:, span], axis=-1, keepdims=True)
            grad_rows[:, span] = (route * grad_f).astype(jnp.bfloat16)
            values = x_buf[:, span].astype(jnp.float32)
            square += jnp.sum(values * values, axis=-1, keepdims=True)
        gate_out[...] = jnp.broadcast_to(gate_grad, gate_out.shape)
        inv_rms = lax.rsqrt(square / width + epsilon)
        grads = []
        for half in range(2):
            side = pl.ds(half * hidden_dim, hidden_dim)
            copies[2][half].wait()
            grad_hidden = product_t(grad_rows[...], down_buf[half])
            gate_pre = pre_gate[:, side]
            sigma = jax.nn.sigmoid(gate_pre)
            grad_gate = grad_hidden * pre_up[:, side] * sigma * (1.0 + gate_pre * (1.0 - sigma))
            grad_up = grad_hidden * gate_pre * sigma
            grads.append((grad_gate.astype(jnp.bfloat16), grad_up.astype(jnp.bfloat16)))
        for half in range(2):
            copies[0][half].wait()
            copies[1][half].wait()
        dotted = jnp.zeros((slots, 1), jnp.float32)
        for span in spans(width, 256):
            total = product_t(grads[0][0], gate_buf[0, span, :])
            total = total + product_t(grads[0][1], up_buf[0, span, :])
            total = total + product_t(grads[1][0], gate_buf[1, span, :])
            total = total + product_t(grads[1][1], up_buf[1, span, :])
            scaled = total * gain_ref[:, span]
            scaled_buf[:, span] = scaled
            dotted += jnp.sum(x_buf[:, span].astype(jnp.float32) * scaled, axis=-1, keepdims=True)
        back = inv_rms * inv_rms * inv_rms * (dotted / width)
        for span in spans(width, 512):
            grad_in = (
                grad_buf[:, span].astype(jnp.float32)
                + inv_rms * scaled_buf[:, span]
                - x_buf[:, span].astype(jnp.float32) * back
            ).astype(jnp.bfloat16)
            for part in range(parts):
                out_refs[part][:, span] = grad_in[part * rows : (part + 1) * rows]


def forward_router(slot, micro_count, parts, has_first, has_rest, *refs):
    sec_ref, place_ref, move_ref = refs[:3]
    rest = refs[3:]
    tokens_ref = rest[0] if has_first else None
    rest = rest[1:] if has_first else rest
    arrived = rest[:parts] if has_rest else None
    rest = rest[parts:] if has_rest else rest
    out_refs = rest[:parts]
    sec = sec_ref[0]
    micro = slot - sec
    width = out_refs[0].shape[1]
    rows = out_refs[0].shape[0]

    def put(table, source):
        for span in spans(width, 512):
            made = product(table, source(span)).astype(jnp.bfloat16)
            for part in range(parts):
                out_refs[part][:, span] = made[part * rows : (part + 1) * rows]

    if has_first:

        @pl.when(sec == 0)
        def _():
            put(place_ref[slot], lambda span: tokens_ref[:, span])

    if has_rest:

        @pl.when((sec > 0) & (micro >= 0) & (micro < micro_count))
        def _():
            put(
                move_ref[micro],
                lambda span: jnp.concatenate([ref[:, span] for ref in arrived], axis=0),
            )


def backward_router(slot, counts, parts, has_former, onward, *refs):
    section_count, micro_count = counts
    sec_ref, take_ref, move_ref = refs[:3]
    arrived = refs[3 : 3 + parts]
    rest = refs[3 + parts + (1 if has_former else 0) :]
    result = rest[0]
    out_refs = rest[1 : 1 + parts] if onward else []
    ordered, sem = rest[1 + len(out_refs) :]
    sec = sec_ref[0]
    micro = slot - 2 * (section_count - 1) + sec
    width = arrived[0].shape[1]
    rows = arrived[0].shape[0]

    @pl.when((micro >= 0) & (micro < micro_count))
    def _():
        def source(span):
            return jnp.concatenate([ref[:, span] for ref in arrived], axis=0)

        if onward:

            @pl.when(sec > 0)
            def _():
                for span in spans(width, 512):
                    made = product(move_ref[micro], source(span)).astype(jnp.bfloat16)
                    for part in range(parts):
                        out_refs[part][:, span] = made[part * rows : (part + 1) * rows]

        for span in spans(width, 512):
            ordered[:, span] = product(take_ref[micro], source(span)).astype(jnp.bfloat16)
        copy = pltpu.make_async_copy(ordered, result.at[micro], sem)
        copy.start()
        copy.wait()


def slots_of(route_ids, expert_count, capacity, turn):
    one_hot = (route_ids[:, :, None] == jnp.arange(expert_count, dtype=jnp.int32)).astype(jnp.int32)
    position = jnp.sum((jnp.cumsum(one_hot, axis=1, dtype=jnp.int32) - 1) * one_hot, axis=-1)
    return lax.rem(route_ids - turn + expert_count, expert_count) * capacity + position


def body(tokens_in, cotangent, norm_gain, w_gate, w_up, w_down, expert_ids, gate_weights):
    section_count = lax.axis_size("section")
    device_count = lax.axis_size("expert")
    section = lax.axis_index("section")
    place = lax.axis_index("expert") // 2
    expert_count = device_count // 2
    micro_count = expert_ids.shape[1]
    tok_rows = expert_ids.shape[2]
    model_dim = tokens_in.shape[2]
    hidden_dim = w_gate.shape[3]
    capacity = 2 * ((tok_rows + expert_count - 1) // expert_count)
    slots = expert_count * capacity
    by_permute = capacity % 16 == 0
    parts = expert_count if by_permute else 1
    rows = slots // parts
    turn = place if by_permute else jnp.int32(0)
    counts = (section_count, micro_count)
    first_back = section_count - 1
    slot_count = micro_count + 2 * (section_count - 1)
    sections = range(section_count)

    def exchange(chunks, jobs, direction):
        if by_permute:
            moved = [None] * parts
            for step in sorted(range(parts), key=lambda k: -min(k, parts - k)):
                if step == 0 and all(a == b for a, b in jobs):
                    moved[0] = chunks[0]
                    continue
                pairs = [
                    (
                        a * device_count + 2 * z + core,
                        b * device_count + 2 * ((z + direction * step) % expert_count) + core,
                    )
                    for a, b in jobs
                    for z in range(expert_count)
                    for core in range(2)
                ]
                moved[step] = lax.ppermute(chunks[step], both, pairs)
            return moved
        (block,) = chunks
        shape = block.shape
        spread = block.reshape(-1, expert_count, capacity, shape[-1])
        groups = [[2 * z + core for z in range(expert_count)] for core in range(2)]
        spread = lax.all_to_all(
            spread, "expert", split_axis=1, concat_axis=1, tiled=True, axis_index_groups=groups
        )
        block = spread.reshape(shape)
        if any(a != b for a, b in jobs):
            block = lax.ppermute(block, "section", jobs)
        return [block]

    def cut(block):
        return [block[:, part * rows : (part + 1) * rows] for part in range(parts)]

    own = (w_gate[0, 0], w_up[0, 0], w_down[0, 0])
    swap = [(i, i ^ 1) for i in range(device_count)]
    other = tuple(lax.ppermute(matrix, "expert", swap) for matrix in own)
    weights = (*own, *other)

    sec = section.reshape(1).astype(jnp.int32)
    gain = norm_gain
    ids = expert_ids[0, :, :, 0]
    former_ids = lax.ppermute(ids, "section", [(s, s + 1) for s in sections[:-1]])
    slot_own = slots_of(ids, expert_count, capacity, turn)
    slot_former = slots_of(former_ids, expert_count, capacity, turn)
    numbers = jnp.arange(slots, dtype=jnp.int32)
    is_own = numbers[None, :, None] == slot_own[:, None, :]
    place_own = is_own.astype(jnp.bfloat16)
    place_former = (numbers[None, :, None] == slot_former[:, None, :]).astype(jnp.bfloat16)
    take_own = place_own.transpose(0, 2, 1)
    move_forward = jnp.einsum("mjt,mit->mji", place_own, place_former)
    move_back = jnp.einsum("mjt,mit->mji", place_former, place_own)
    route_slots = jnp.sum(jnp.where(is_own, gate_weights[0, :, None, :, 0], 0.0), axis=-1)
    route_parts = exchange(cut(route_slots[:, :, None]), [(s, s) for s in sections], 1)
    route = jnp.concatenate(route_parts, axis=1)

    tokens_all = [tokens_in[0]]
    cotangent_all = []
    for step in range(1, section_count):
        sent = jnp.where(section == step, tokens_in[0], cotangent[0])
        came = lax.ppermute(sent, "section", [(step, 0), (step - 1, section_count - 1)])
        tokens_all.append(came)
        cotangent_all.append(came)
    cotangent_all.append(cotangent[0])
    packed = jnp.einsum(
        "mjt,mtd->mjd", place_own, jnp.stack(cotangent_all), preferred_element_type=jnp.float32
    ).astype(jnp.bfloat16)
    first_grads = exchange(cut(packed), [(first_back, first_back)], 1)

    chunk = jax.ShapeDtypeStruct((rows, model_dim), jnp.bfloat16)
    weight_scratch = [
        pltpu.VMEM((2, model_dim, hidden_dim), jnp.bfloat16),
        pltpu.VMEM((2, model_dim, hidden_dim), jnp.bfloat16),
        pltpu.VMEM((2, hidden_dim, model_dim), jnp.bfloat16),
    ]
    weight_bytes = 6 * model_dim * hidden_dim * 2
    flops = 2 * slots * 6 * model_dim * hidden_dim
    heavy = pl.CostEstimate(flops=flops, bytes_accessed=weight_bytes, transcendentals=0)
    state_shapes = [
        jax.ShapeDtypeStruct((slots, model_dim), jnp.bfloat16),
        jax.ShapeDtypeStruct((slots, 2 * hidden_dim), jnp.float32),
        jax.ShapeDtypeStruct((slots, 2 * hidden_dim), jnp.float32),
        jax.ShapeDtypeStruct((slots, model_dim), jnp.float32),
    ]

    saved = {}
    ahead = None
    behind = None
    gate_slots = []
    result = None
    for slot in range(slot_count):
        forward_on = [s for s in sections if 0 <= slot - s < micro_count]
        if forward_on:
            has_first = 0 in forward_on
            has_rest = ahead is not None
            packed = pl.pallas_call(
                partial(forward_router, slot, micro_count, parts, has_first, has_rest),
                out_shape=[chunk] * parts,
                in_specs=[in_smem, in_vmem, in_vmem]
                + [in_vmem] * ((1 if has_first else 0) + (parts if has_rest else 0)),
                out_specs=[in_vmem] * parts,
                compiler_params=params(16),
                name=f"route_forward_{slot}",
            )(
                sec,
                place_own,
                move_forward,
                *([tokens_all[slot]] if has_first else []),
                *(ahead if has_rest else []),
            )
            moved = exchange(packed, [(s, s) for s in forward_on], 1)
            outs = pl.pallas_call(
                partial(forward_kernel, slot, micro_count, parts),
                out_shape=[chunk] * parts + state_shapes,
                in_specs=[in_smem, in_vmem, in_vmem] + [in_vmem] * parts + [anywhere] * 6,
                out_specs=[in_vmem] * (parts + 4),
                scratch_shapes=weight_scratch
                + [
                    pltpu.VMEM((slots, model_dim), jnp.bfloat16),
                    pltpu.VMEM((2, slots, hidden_dim), jnp.bfloat16),
                    pltpu.SemaphoreType.DMA((3, 2)),
                ],
                compiler_params=params(40),
                cost_estimate=heavy,
                name=f"expert_forward_{slot}",
            )(sec, gain, route, *moved, *weights)
            x_rows, pre_gate, pre_up, made = outs[parts:]
            saved[slot] = (made, x_rows, pre_gate, pre_up)
            jobs = [(s, s + 1) for s in forward_on if s + 1 < section_count]
            ahead = exchange(outs[:parts], jobs, -1) if jobs else None
        backward_on = [s for s in sections if 0 <= slot - 2 * first_back + s < micro_count]
        if backward_on:
            jobs = [(s + 1, s) for s in backward_on if s < first_back]
            grads = exchange(behind, jobs, 1) if jobs else [part[0] for part in first_grads]
            states = []
            for s in backward_on:
                states += list(saved[slot - 2 * first_back + 2 * s])
            outs = pl.pallas_call(
                partial(backward_kernel, slot, counts, backward_on, parts),
                out_shape=[chunk] * parts + [jax.ShapeDtypeStruct((slots, 128), jnp.float32)],
                in_specs=[in_smem, in_vmem, in_vmem]
                + [anywhere] * (2 * parts + 6 + len(states)),
                out_specs=[in_vmem] * (parts + 1),
                scratch_shapes=weight_scratch
                + [
                    pltpu.VMEM((slots, model_dim), jnp.bfloat16),
                    pltpu.VMEM((slots, model_dim), jnp.bfloat16),
                    pltpu.VMEM((slots, 2 * hidden_dim), jnp.float32),
                    pltpu.VMEM((slots, 2 * hidden_dim), jnp.float32),
                    pltpu.VMEM((slots, model_dim), jnp.float32),
                    pltpu.VMEM((slots, model_dim), jnp.bfloat16),
                    pltpu.VMEM((slots, model_dim), jnp.float32),
                    pltpu.SemaphoreType.DMA((3, 2)),
                    pltpu.SemaphoreType.DMA((4,)),
                    pltpu.SemaphoreType.DMA((parts,)),
                ],
                compiler_params=params(40),
                cost_estimate=heavy,
                name=f"expert_backward_{slot}",
            )(sec, gain, route, *grads, *first_grads, *weights, *states)
            gate_slots.append(outs[parts][:, 0])
            home = exchange(outs[:parts], [(s, s) for s in backward_on], -1)
            onward = slot + 1 < slot_count
            has_former = result is not None
            outs = pl.pallas_call(
                partial(backward_router, slot, counts, parts, has_former, onward),
                out_shape=[jax.ShapeDtypeStruct((micro_count, tok_rows, model_dim), jnp.bfloat16)]
                + [chunk] * (parts if onward else 0),
                in_specs=[in_smem, in_vmem, in_vmem]
                + [in_vmem] * parts
                + [anywhere] * (1 if has_former else 0),
                out_specs=[anywhere] + [in_vmem] * (parts if onward else 0),
                scratch_shapes=[
                    pltpu.VMEM((tok_rows, model_dim), jnp.bfloat16),
                    pltpu.SemaphoreType.DMA,
                ],
                input_output_aliases={3 + parts: 0} if has_former else {},
                compiler_params=params(16),
                name=f"route_backward_{slot}",
            )(sec, take_own, move_back, *home, *([result] if has_former else []))
            result = outs[0]
            behind = outs[1:]

    gates = lax.dynamic_slice_in_dim(jnp.stack(gate_slots), first_back - section, micro_count, 0)
    gate_parts = exchange(cut(gates[:, :, None]), [(s, s) for s in sections], -1)
    gates = jnp.concatenate(gate_parts, axis=1)
    gate_out = jnp.sum(jnp.where(is_own, gates, 0.0), axis=1)
    return (result[None], gate_out[None, :, :, None])


def solution(mesh):
    return jax.shard_map(
        body,
        mesh=mesh,
        in_specs=(
            P("section", "expert", None),
            P("section", "expert", None),
            P("section", None),
            P("section", "expert", None, None),
            P("section", "expert", None, None),
            P("section", "expert", None, None),
            P("section", None, "expert", None),
            P("section", None, "expert", None),
        ),
        out_specs=(P("section", None, "expert", None), P("section", None, "expert", None)),
        check_vma=False,
    )
```

time: 1870 us -> 682 us (0.36)
  waiting for transfers between devices: 640 us -> 120 us
  other arithmetic: 511 us -> 6.36 us
  local copies, waits for them, and re-layouts: 414 us -> 37.9 us
  starting transfers between devices: 159 us -> 421 us
  Pallas kernels: 0 us -> 82 us
  matrix products: 61.5 us -> 1.12 us
  loops' own time: 34.5 us -> 0 us
  blocking collectives: 31 us -> 0 us
    all_to_all x28 -> x0, waiting for transfers between devices: 515 us -> none  [the longest x14 271 us: collect(): lax.all_to_all(flat_rows, 'expert', split_axis=0, concat_axis=0, tiled=True)]
    ppermute x12 -> x106, starting transfers between devices: 44.3 us -> 421 us  [the longest x99 383 us: exchange(): moved[step] = lax.ppermute(chunks[step], both, pairs)]
    all_to_all x28 -> x0, other arithmetic: 216 us -> none  [the longest x14 108 us: collect(): lax.all_to_all(flat_rows, 'expert', split_axis=0, concat_axis=0, tiled=True)]
    unnamed x181 -> x190, local copies, waits for them, and re-layouts: 182 us -> 36.7 us
    convert_element_type x21 -> x4, other arithmetic: 118 us -> 0.95 us  [the longest x2 0.85 us: slots_of(): (route_ids[:, :, None] == jnp.arange(expert_count, dtype=jnp.int32)).asty...]
    all_to_all x28 -> x0, starting transfers between devices: 115 us -> none  [the longest x14 58.3 us: collect(): lax.all_to_all(flat_rows, 'expert', split_axis=0, concat_axis=0, tiled=True)]
    pallas_call x0 -> x28, Pallas kernels: none -> 82 us  [the longest x7 49.5 us: body(): pl.pallas_call(partial(backward_kernel, slot, counts, backward_on, parts)...]
    all_to_all x29 -> x0, local copies, waits for them, and re-layouts: 71.9 us -> none  [the longest x15 38.3 us: dispatch(): lax.all_to_all(doubled, 'expert', split_axis=0, concat_axis=0, tiled=True)]
  transfers between devices with their start and end apart: 40 -> 106, of which waited for: 38 -> 35; matrix products, arithmetic and copies ran while one was open for 8% -> 1% of each run, Pallas kernels for 0% -> 3%
where the time goes in v1:
time: 682 us; the launch traced here: 672 us
  starting transfers between devices  421 us (62%)
  waiting for transfers between devices  120 us (18%)
  Pallas kernels  82 us (12%)
  local copies, waits for them, and re-layouts  37.9 us (6%)
    ppermute x99, starting transfers between devices, exchange(): moved[step] = lax.ppermute(chunks[step], both, pairs)  383 us
    ppermute x99, waiting for transfers between devices, exchange(): moved[step] = lax.ppermute(chunks[step], both, pairs)  120 us
    pallas_call x7, Pallas kernels, body(): pl.pallas_call(partial(backward_kernel, slot, counts, backward_on, parts)...  49.5 us
    unnamed x190, local copies, waits for them, and re-layouts  36.7 us
    pallas_call x7, Pallas kernels, body(): pl.pallas_call(partial(forward_kernel, slot, micro_count, parts), out_sha...  26.8 us
    ppermute x3, starting transfers between devices, body(): other = tuple((lax.ppermute(matrix, 'expert', swap) for matrix in own))  18.6 us
    ppermute x3, starting transfers between devices, body(): lax.ppermute(sent, 'section', [(step, 0), (step - 1, section_count - 1)])  15.5 us
  transfers between devices with their start and end apart: 106, of which 35 were waited for; matrix products, arithmetic and copies ran while one was open for 1% of the time, Pallas kernels for 3%

profile of v1, /device:TPU:0, one launch (start us, length us, event | category | flops | bytes accessed | tf_op | source)
XLA Modules:
  0.0 672.3 jit_solution(8141832299580081956)
XLA Ops:
  0.6 7.1 %collective-permute-start.10 = (bf16[3584,512]{1,0:T(8,128)(2,1)}, bf16[3584,512]{1,0:T(8,128)(2,1)}, u32[]{:S(2)}, u32[]{:S(2)}) collective-permute-start(bf16[3584,512]{1,0:T(8,128)(2,1)} %bitcast.41), channel_id=1, source_target_pairs={{0,1},{1,0},{2,3},{3,2},{4,5},{5,4},{6,7},{7,6},{8,9},{9,8},{10,11... | collective-permute-start | bytes 11010056 | tf_op jit(solution)/shard_map/ppermute | solution.py:325
  7.8 5.7 collective-permute-start.11
  13.5 5.7 collective-permute-start.12
  57.2 5.7 collective-permute-start.5
  62.9 6.3 collective-permute-start.6
  76.3 6.5 expert_forward_0.1
  110.7 6.3 expert_forward_1.1
  117.0 7.3 %collective-permute-start.23 = (bf16[16,3584]{1,0:T(8,128)(2,1)S(1)}, bf16[16,3584]{1,0:T(8,128)(2,1)S(1)}, u32[]{:S(2)}, u32[]{:S(2)}) collective-permute-start(bf16[16,3584]{1,0:T(8,128)(2,1)S(1)} %get-tuple-element.159), channel_id=1, source_target_pairs={{0,8},{1,9},{2,10},{3,11},{4,12},{5,13},{6,14},{7,15},{8,16},{9,17... | collective-permute-start | bytes 344072 | tf_op jit(solution)/shard_map/ppermute | solution.py:306
  124.3 6.4 collective-permute-start.24
  130.7 6.4 collective-permute-start.25
  137.1 6.4 collective-permute-start.26
  162.2 6.7 expert_forward_2.1
  169.0 6.9 %collective-permute-start.30 = (bf16[16,3584]{1,0:T(8,128)(2,1)S(1)}, bf16[16,3584]{1,0:T(8,128)(2,1)S(1)}, u32[]{:S(2)}, u32[]{:S(2)}) collective-permute-start(bf16[16,3584]{1,0:T(8,128)(2,1)S(1)} %get-tuple-element.167), channel_id=1, source_target_pairs={{0,8},{1,9},{2,10},{3,11},{4,12},{5,13},{6,14},{7,15},{8,16},{9,17... | collective-permute-start | bytes 344072 | tf_op jit(solution)/shard_map/ppermute | solution.py:306
  200.8 6.2 expert_forward_3.1
  208.6 6.5 collective-permute-start.44
  215.1 6.2 collective-permute-start.45
  221.3 11.7 %collective-permute-start.46 = (bf16[16,3584]{1,0:T(8,128)(2,1)S(1)}, bf16[16,3584]{1,0:T(8,128)(2,1)S(1)}, u32[]{:S(2)}, u32[]{:S(2)}) collective-permute-start(bf16[16,3584]{1,0:T(8,128)(2,1)S(1)} %get-tuple-element.193), channel_id=1, source_target_pairs={{0,12},{1,13},{2,14},{3,15},{4,8},{5,9},{6,10},{7,11},{8,20},{9,21... | collective-permute-start | bytes 344072 | tf_op jit(solution)/shard_map/ppermute | solution.py:306
  242.2 14.6 %collective-permute-start.40 = (bf16[16,3584]{1,0:T(8,128)(2,1)S(1)}, bf16[16,3584]{1,0:T(8,128)(2,1)S(1)}, u32[]{:S(2)}, u32[]{:S(2)}) collective-permute-start(bf16[16,3584]{1,0:T(8,128)(2,1)S(1)} %get-tuple-element.183), channel_id=1, source_target_pairs={{24,16},{25,17},{26,18},{27,19},{28,20},{29,21},{30,22},{31,23}} | collective-permute-start | bytes 344072 | tf_op jit(solution)/shard_map/ppermute | solution.py:306
  256.7 7.0 %collective-permute-start.41 = (bf16[16,3584]{1,0:T(8,128)(2,1)S(1)}, bf16[16,3584]{1,0:T(8,128)(2,1)S(1)}, u32[]{:S(2)}, u32[]{:S(2)}) collective-permute-start(bf16[16,3584]{1,0:T(8,128)(2,1)S(1)} %get-tuple-element.184), channel_id=1, source_target_pairs={{24,18},{25,19},{26,20},{27,21},{28,22},{29,23},{30,16},{31,17}} | collective-permute-start | bytes 344072 | tf_op jit(solution)/shard_map/ppermute | solution.py:306
  263.8 7.0 %collective-permute-start.42 = (bf16[16,3584]{1,0:T(8,128)(2,1)S(1)}, bf16[16,3584]{1,0:T(8,128)(2,1)S(1)}, u32[]{:S(2)}, u32[]{:S(2)}) collective-permute-start(bf16[16,3584]{1,0:T(8,128)(2,1)S(1)} %get-tuple-element.185), channel_id=1, source_target_pairs={{24,20},{25,21},{26,22},{27,23},{28,16},{29,17},{30,18},{31,19}} | collective-permute-start | bytes 344072 | tf_op jit(solution)/shard_map/ppermute | solution.py:306
  270.8 7.0 %collective-permute-start.43 = (bf16[16,3584]{1,0:T(8,128)(2,1)S(1)}, bf16[16,3584]{1,0:T(8,128)(2,1)S(1)}, u32[]{:S(2)}, u32[]{:S(2)}) collective-permute-start(bf16[16,3584]{1,0:T(8,128)(2,1)S(1)} %get-tuple-element.186), channel_id=1, source_target_pairs={{24,22},{25,23},{26,16},{27,17},{28,18},{29,19},{30,20},{31,21}} | collective-permute-start | bytes 344072 | tf_op jit(solution)/shard_map/ppermute | solution.py:306
  278.1 13.2 %collective-permute-start.58 = (bf16[16,3584]{1,0:T(8,128)(2,1)S(1)}, bf16[16,3584]{1,0:T(8,128)(2,1)S(1)}, u32[]{:S(2)}, u32[]{:S(2)}) collective-permute-start(bf16[16,3584]{1,0:T(8,128)(2,1)S(1)} %get-tuple-element.216), channel_id=1, source_target_pairs={{8,16},{9,17},{10,18},{11,19},{12,20},{13,21},{14,22},{15,23},{16,... | collective-permute-start | bytes 344072 | tf_op jit(solution)/shard_map/ppermute | solution.py:306
  291.3 6.3 collective-permute-start.59
  297.7 6.3 collective-permute-start.60
  304.1 6.3 collective-permute-start.61
  311.5 19.3 %collective-permute-start.52 = (bf16[16,3584]{1,0:T(8,128)(2,1)S(1)}, bf16[16,3584]{1,0:T(8,128)(2,1)S(1)}, u32[]{:S(2)}, u32[]{:S(2)}) collective-permute-start(bf16[16,3584]{1,0:T(8,128)(2,1)S(1)} %get-tuple-element.205), channel_id=1, source_target_pairs={{16,20},{17,21},{18,22},{19,23},{20,16},{21,17},{22,18},{23,19},{2... | collective-permute-start | bytes 344072 | tf_op jit(solution)/shard_map/ppermute | solution.py:306
  330.8 7.0 %collective-permute-start.53 = (bf16[16,3584]{1,0:T(8,128)(2,1)S(1)}, bf16[16,3584]{1,0:T(8,128)(2,1)S(1)}, u32[]{:S(2)}, u32[]{:S(2)}) collective-permute-start(bf16[16,3584]{1,0:T(8,128)(2,1)S(1)} %get-tuple-element.206), channel_id=1, source_target_pairs={{16,18},{17,19},{18,20},{19,21},{20,22},{21,23},{22,16},{23,17},{2... | collective-permute-start | bytes 344072 | tf_op jit(solution)/shard_map/ppermute | solution.py:306
  337.9 7.3 %collective-permute-start.62 = (bf16[16,3584]{1,0:T(8,128)(2,1)S(1)}, bf16[16,3584]{1,0:T(8,128)(2,1)S(1)}, u32[]{:S(2)}, u32[]{:S(2)}) collective-permute-start(bf16[16,3584]{1,0:T(8,128)(2,1)S(1)} %get-tuple-element.221), channel_id=1, source_target_pairs={{16,18},{17,19},{18,20},{19,21},{20,22},{21,23},{22,16},{23,17},{2... | collective-permute-start | bytes 344072 | tf_op jit(solution)/shard_map/ppermute | solution.py:306
  345.1 7.0 %collective-permute-start.63 = (bf16[16,3584]{1,0:T(8,128)(2,1)S(1)}, bf16[16,3584]{1,0:T(8,128)(2,1)S(1)}, u32[]{:S(2)}, u32[]{:S(2)}) collective-permute-start(bf16[16,3584]{1,0:T(8,128)(2,1)S(1)} %get-tuple-element.222), channel_id=1, source_target_pairs={{16,20},{17,21},{18,22},{19,23},{20,16},{21,17},{22,18},{23,19},{2... | collective-permute-start | bytes 344072 | tf_op jit(solution)/shard_map/ppermute | solution.py:306
  352.9 10.0 %collective-permute-start.54 = (bf16[16,3584]{1,0:T(8,128)(2,1)S(1)}, bf16[16,3584]{1,0:T(8,128)(2,1)S(1)}, u32[]{:S(2)}, u32[]{:S(2)}) collective-permute-start(bf16[16,3584]{1,0:T(8,128)(2,1)S(1)} %get-tuple-element.208), channel_id=1, source_target_pairs={{16,8},{17,9},{18,10},{19,11},{20,12},{21,13},{22,14},{23,15},{24,... | collective-permute-start | bytes 344072 | tf_op jit(solution)/shard_map/ppermute | solution.py:306
  362.9 7.0 %collective-permute-start.55 = (bf16[16,3584]{1,0:T(8,128)(2,1)S(1)}, bf16[16,3584]{1,0:T(8,128)(2,1)S(1)}, u32[]{:S(2)}, u32[]{:S(2)}) collective-permute-start(bf16[16,3584]{1,0:T(8,128)(2,1)S(1)} %get-tuple-element.209), channel_id=1, source_target_pairs={{16,10},{17,11},{18,12},{19,13},{20,14},{21,15},{22,8},{23,9},{24,... | collective-permute-start | bytes 344072 | tf_op jit(solution)/shard_map/ppermute | solution.py:306
  369.9 7.0 %collective-permute-start.56 = (bf16[16,3584]{1,0:T(8,128)(2,1)S(1)}, bf16[16,3584]{1,0:T(8,128)(2,1)S(1)}, u32[]{:S(2)}, u32[]{:S(2)}) collective-permute-start(bf16[16,3584]{1,0:T(8,128)(2,1)S(1)} %get-tuple-element.210), channel_id=1, source_target_pairs={{16,12},{17,13},{18,14},{19,15},{20,8},{21,9},{22,10},{23,11},{24,... | collective-permute-start | bytes 344072 | tf_op jit(solution)/shard_map/ppermute | solution.py:306
  376.9 7.0 %collective-permute-start.57 = (bf16[16,3584]{1,0:T(8,128)(2,1)S(1)}, bf16[16,3584]{1,0:T(8,128)(2,1)S(1)}, u32[]{:S(2)}, u32[]{:S(2)}) collective-permute-start(bf16[16,3584]{1,0:T(8,128)(2,1)S(1)} %get-tuple-element.211), channel_id=1, source_target_pairs={{16,14},{17,15},{18,8},{19,9},{20,10},{21,11},{22,12},{23,13},{24,... | collective-permute-start | bytes 344072 | tf_op jit(solution)/shard_map/ppermute | solution.py:306
  384.8 15.0 %collective-permute-start.73 = (bf16[16,3584]{1,0:T(8,128)(2,1)S(1)}, bf16[16,3584]{1,0:T(8,128)(2,1)S(1)}, u32[]{:S(2)}, u32[]{:S(2)}) collective-permute-start(bf16[16,3584]{1,0:T(8,128)(2,1)S(1)} %get-tuple-element.242), channel_id=1, source_target_pairs={{16,30},{17,31},{18,24},{19,25},{20,26},{21,27},{22,28},{23,29}} | collective-permute-start | bytes 344072 | tf_op jit(solution)/shard_map/ppermute | solution.py:306
  399.8 6.3 collective-permute-start.74
  406.2 6.3 collective-permute-start.75
  427.0 23.1 %collective-permute-done.68.refs_3_ = bf16[16,3584]{1,0:T(8,128)(2,1)S(1)} collective-permute-done((bf16[16,3584]{1,0:T(8,128)(2,1)S(1)}, bf16[16,3584]{1,0:T(8,128)(2,1)S(1)}, u32[]{:S(2)}, u32[]{:S(2)}) %collective-permute-start.68) | collective-permute-done | bytes 114720 | tf_op jit(solution)/shard_map/ppermute | solution.py:306
  466.0 12.4 %expert_backward_6.1 = (bf16[16,3584]{1,0:T(8,128)(2,1)S(1)}, bf16[16,3584]{1,0:T(8,128)(2,1)S(1)}, bf16[16,3584]{1,0:T(8,128)(2,1)S(1)}, bf16[16,3584]{1,0:T(8,128)(2,1)S(1)}, f32[64,128]{1,0:T(8,128)S(1)}) custom-call(s32[1]{0:T(128)} %bitcast.refs_0_, f32[1,3584]{1,0:T(1,128)S(1)} %copy-done.33, f32[4,64,1]{2,1,0:T(8,128)S(1)} %copy.44.refs_2_, ...), custom_call_target="tpu_custom_call" | custom-call | flops 1409286144 | bytes 22020096 | tf_op jit(solution)/shard_map/expert_backward_6/pallas_call | solution.py:426
  485.2 7.9 %collective-permute-done.80.refs_5_ = bf16[16,3584]{1,0:T(8,128)(2,1)S(1)} collective-permute-done((bf16[16,3584]{1,0:T(8,128)(2,1)S(1)}, bf16[16,3584]{1,0:T(8,128)(2,1)S(1)}, u32[]{:S(2)}, u32[]{:S(2)}) %collective-permute-start.80) | collective-permute-done | bytes 114720 | tf_op jit(solution)/shard_map/ppermute | solution.py:306
  510.4 13.6 %expert_backward_7.1 = (bf16[16,3584]{1,0:T(8,128)(2,1)S(1)}, bf16[16,3584]{1,0:T(8,128)(2,1)}, bf16[16,3584]{1,0:T(8,128)(2,1)}, bf16[16,3584]{1,0:T(8,128)(2,1)}, f32[64,128]{1,0:T(8,128)S(1)}) custom-call(s32[1]{0:T(128)} %bitcast.refs_0_, f32[1,3584]{1,0:T(1,128)S(1)} %copy-done.33, f32[4,64,1]{2,1,0:T(8,128)S(1)} %copy.44.refs_2_, ...), custom_call_target="tpu_custom_call" | custom-call | flops 1409286144 | bytes 22020096 | tf_op jit(solution)/shard_map/expert_backward_7/pallas_call | solution.py:426
  535.0 5.6 collective-permute-done.87.refs_5_
  544.6 8.1 %collective-permute-start.89 = (bf16[16,3584]{1,0:T(8,128)(2,1)S(1)}, bf16[16,3584]{1,0:T(8,128)(2,1)S(1)}, u32[]{:S(2)}, u32[]{:S(2)}) collective-permute-start(bf16[16,3584]{1,0:T(8,128)(2,1)S(1)} %get-tuple-element.267), channel_id=1, source_target_pairs={{8,0},{9,1},{10,2},{11,3},{12,4},{13,5},{14,6},{15,7},{16,8},{17,9... | collective-permute-start | bytes 344072 | tf_op jit(solution)/shard_map/ppermute | solution.py:306
  552.8 6.4 collective-permute-start.90
  559.2 6.4 collective-permute-start.91
  565.5 6.4 collective-permute-start.92
  591.1 11.3 %expert_backward_8.1 = (bf16[16,3584]{1,0:T(8,128)(2,1)S(1)}, bf16[16,3584]{1,0:T(8,128)(2,1)S(1)}, bf16[16,3584]{1,0:T(8,128)(2,1)S(1)}, bf16[16,3584]{1,0:T(8,128)(2,1)S(1)}, f32[64,128]{1,0:T(8,128)S(1)}) custom-call(s32[1]{0:T(128)} %bitcast.refs_0_, f32[1,3584]{1,0:T(1,128)S(1)} %copy-done.34, f32[4,64,1]{2,1,0:T(8,128)S(1)} %copy.44.refs_2_, ...), custom_call_target="tpu_custom_call" | custom-call | flops 1409286144 | bytes 22020096 | tf_op jit(solution)/shard_map/expert_backward_8/pallas_call | solution.py:426
  635.2 11.4 %expert_backward_9.1 = (bf16[16,3584]{1,0:T(8,128)(2,1)S(1)}, bf16[16,3584]{1,0:T(8,128)(2,1)S(1)}, bf16[16,3584]{1,0:T(8,128)(2,1)S(1)}, bf16[16,3584]{1,0:T(8,128)(2,1)S(1)}, f32[64,128]{1,0:T(8,128)S(1)}) custom-call(s32[1]{0:T(128)} %bitcast.refs_0_, f32[1,3584]{1,0:T(1,128)S(1)} %copy-done.34, f32[4,64,1]{2,1,0:T(8,128)S(1)} %copy.44.refs_2_, ...), custom_call_target="tpu_custom_call" | custom-call | flops 1409286144 | bytes 22020096 | tf_op jit(solution)/shard_map/expert_backward_9/pallas_call | solution.py:426
  663.9 6.4 collective-permute-done.101.refs_5_
  (417 shorter events, 268.8 us)
Async XLA Ops:
  0.6 62.3 %collective-permute-start.10 = (bf16[3584,512]{1,0:T(8,128)(2,1)}, bf16[3584,512]{1,0:T(8,128)(2,1)}, u32[]{:S(2)}, u32[]{:S(2)}) collective-permute-start(bf16[3584,512]{1,0:T(8,128)(2,1)} %bitcast.41), channel_id=1, source_target_pairs={{0,1},{1,0},{2,3},{3,2},{4,5},{5,4},{6,7},{7,6},{8,9},{9,8},{10,11... | collective-permute-start | bytes 11010056 | tf_op jit(solution)/shard_map/ppermute | solution.py:325
  7.8 61.7 %collective-permute-start.11 = (bf16[3584,512]{1,0:T(8,128)(2,1)}, bf16[3584,512]{1,0:T(8,128)(2,1)}, u32[]{:S(2)}, u32[]{:S(2)}) collective-permute-start(bf16[3584,512]{1,0:T(8,128)(2,1)} %bitcast.56), channel_id=1, source_target_pairs={{0,1},{1,0},{2,3},{3,2},{4,5},{5,4},{6,7},{7,6},{8,9},{9,8},{10,11... | collective-permute-start | bytes 11010056 | tf_op jit(solution)/shard_map/ppermute | solution.py:325
  13.5 56.0 %collective-permute-start.12 = (bf16[512,3584]{1,0:T(8,128)(2,1)}, bf16[512,3584]{1,0:T(8,128)(2,1)}, u32[]{:S(2)}, u32[]{:S(2)}) collective-permute-start(bf16[512,3584]{1,0:T(8,128)(2,1)} %bitcast.71), channel_id=1, source_target_pairs={{0,1},{1,0},{2,3},{3,2},{4,5},{5,4},{6,7},{7,6},{8,9},{9,8},{10,11... | collective-permute-start | bytes 11010056 | tf_op jit(solution)/shard_map/ppermute | solution.py:325
  28.1 19.5 %collective-permute-start.13 = (bf16[16,3584]{1,0:T(8,128)(2,1)S(1)}, bf16[16,3584]{1,0:T(8,128)(2,1)S(1)}, u32[]{:S(2)}, u32[]{:S(2)}) collective-permute-start(bf16[16,3584]{1,0:T(8,128)(2,1)S(1)} %get-tuple-element.148), channel_id=1, source_target_pairs={{0,2},{1,3},{2,4},{3,5},{4,6},{5,7},{6,0},{7,1}} | collective-permute-start | bytes 344072 | tf_op jit(solution)/shard_map/ppermute | solution.py:306
  53.7 31.7 %collective-permute-start.4 = (bf16[32,3584]{1,0:T(8,128)(2,1)}, bf16[32,3584]{1,0:T(8,128)(2,1)S(1)}, u32[]{:S(2)}, u32[]{:S(2)}) collective-permute-start(bf16[32,3584]{1,0:T(8,128)(2,1)} %get-tuple-element.302), channel_id=1, source_target_pairs={{8,0},{0,24},{9,1},{1,25},{10,2},{2,26},{11,3},{3,27},{12,4},{4,28... | collective-permute-start | bytes 688136 | tf_op jit(solution)/shard_map/ppermute | solution.py:349
  57.2 29.6 %collective-permute-start.5 = (bf16[32,3584]{1,0:T(8,128)(2,1)S(1)}, bf16[32,3584]{1,0:T(8,128)(2,1)S(1)}, u32[]{:S(2)}, u32[]{:S(2)}) collective-permute-start(bf16[32,3584]{1,0:T(8,128)(2,1)S(1)} %get-tuple-element.303), channel_id=1, source_target_pairs={{16,0},{8,24},{17,1},{9,25},{18,2},{10,26},{19,3},{11,27},{20,4},{... | collective-permute-start | bytes 688136 | tf_op jit(solution)/shard_map/ppermute | solution.py:349
  62.9 25.2 %collective-permute-start.6 = (bf16[32,3584]{1,0:T(8,128)(2,1)S(1)}, bf16[32,3584]{1,0:T(8,128)(2,1)S(1)}, u32[]{:S(2)}, u32[]{:S(2)}) collective-permute-start(bf16[32,3584]{1,0:T(8,128)(2,1)S(1)} %get-tuple-element.304), channel_id=1, source_target_pairs={{24,0},{16,24},{25,1},{17,25},{26,2},{18,26},{27,3},{19,27},{28,4}... | collective-permute-start | bytes 688136 | tf_op jit(solution)/shard_map/ppermute | solution.py:349
  107.7 47.1 %collective-permute-start.9 = (bf16[4,16,3584]{2,1,0:T(8,128)(2,1)S(1)}, bf16[4,16,3584]{2,1,0:T(8,128)(2,1)S(1)}, u32[]{:S(2)}, u32[]{:S(2)}) collective-permute-start(bf16[4,16,3584]{2,1,0:T(8,128)(2,1)S(1)} %get-tuple-element.299), channel_id=1, source_target_pairs={{24,30},{25,31},{26,24},{27,25},{28,26},{29,27},{30,28},{31,29}} | collective-permute-start | bytes 1376264 | tf_op jit(solution)/shard_map/ppermute | solution.py:306
  117.0 26.5 %collective-permute-start.23 = (bf16[16,3584]{1,0:T(8,128)(2,1)S(1)}, bf16[16,3584]{1,0:T(8,128)(2,1)S(1)}, u32[]{:S(2)}, u32[]{:S(2)}) collective-permute-start(bf16[16,3584]{1,0:T(8,128)(2,1)S(1)} %get-tuple-element.159), channel_id=1, source_target_pairs={{0,8},{1,9},{2,10},{3,11},{4,12},{5,13},{6,14},{7,15},{8,16},{9,17... | collective-permute-start | bytes 344072 | tf_op jit(solution)/shard_map/ppermute | solution.py:306
  124.3 19.9 %collective-permute-start.24 = (bf16[16,3584]{1,0:T(8,128)(2,1)S(1)}, bf16[16,3584]{1,0:T(8,128)(2,1)S(1)}, u32[]{:S(2)}, u32[]{:S(2)}) collective-permute-start(bf16[16,3584]{1,0:T(8,128)(2,1)S(1)} %get-tuple-element.160), channel_id=1, source_target_pairs={{0,14},{1,15},{2,8},{3,9},{4,10},{5,11},{6,12},{7,13},{8,22},{9,23... | collective-permute-start | bytes 344072 | tf_op jit(solution)/shard_map/ppermute | solution.py:306
  143.5 40.5 %collective-permute-start.8 = (bf16[4,16,3584]{2,1,0:T(8,128)(2,1)S(1)}, bf16[4,16,3584]{2,1,0:T(8,128)(2,1)S(1)}, u32[]{:S(2)}, u32[]{:S(2)}) collective-permute-start(bf16[4,16,3584]{2,1,0:T(8,128)(2,1)S(1)} %get-tuple-element.300), channel_id=1, source_target_pairs={{24,28},{25,29},{26,30},{27,31},{28,24},{29,25},{30,26},{31,27}} | collective-permute-start | bytes 1376264 | tf_op jit(solution)/shard_map/ppermute | solution.py:306
  144.2 52.5 %collective-permute-start.7 = (bf16[4,16,3584]{2,1,0:T(8,128)(2,1)S(1)}, bf16[4,16,3584]{2,1,0:T(8,128)(2,1)S(1)}, u32[]{:S(2)}, u32[]{:S(2)}) collective-permute-start(bf16[4,16,3584]{2,1,0:T(8,128)(2,1)S(1)} %get-tuple-element.301), channel_id=1, source_target_pairs={{24,26},{25,27},{26,28},{27,29},{28,30},{29,31},{30,24},{31,25}} | collective-permute-start | bytes 1376264 | tf_op jit(solution)/shard_map/ppermute | solution.py:306
  169.0 16.3 %collective-permute-start.30 = (bf16[16,3584]{1,0:T(8,128)(2,1)S(1)}, bf16[16,3584]{1,0:T(8,128)(2,1)S(1)}, u32[]{:S(2)}, u32[]{:S(2)}) collective-permute-start(bf16[16,3584]{1,0:T(8,128)(2,1)S(1)} %get-tuple-element.167), channel_id=1, source_target_pairs={{0,8},{1,9},{2,10},{3,11},{4,12},{5,13},{6,14},{7,15},{8,16},{9,17... | collective-permute-start | bytes 344072 | tf_op jit(solution)/shard_map/ppermute | solution.py:306
  207.8 33.4 %collective-permute-start.37 = (bf16[16,3584]{1,0:T(8,128)(2,1)S(1)}, bf16[16,3584]{1,0:T(8,128)(2,1)S(1)}, u32[]{:S(2)}, u32[]{:S(2)}) collective-permute-start(bf16[16,3584]{1,0:T(8,128)(2,1)S(1)} %get-tuple-element.180), channel_id=1, source_target_pairs={{24,30},{25,31},{26,24},{27,25},{28,26},{29,27},{30,28},{31,29}} | collective-permute-start | bytes 344072 | tf_op jit(solution)/shard_map/ppermute | solution.py:306
  208.6 28.8 %collective-permute-start.44 = (bf16[16,3584]{1,0:T(8,128)(2,1)S(1)}, bf16[16,3584]{1,0:T(8,128)(2,1)S(1)}, u32[]{:S(2)}, u32[]{:S(2)}) collective-permute-start(bf16[16,3584]{1,0:T(8,128)(2,1)S(1)} %get-tuple-element.191), channel_id=1, source_target_pairs={{0,8},{1,9},{2,10},{3,11},{4,12},{5,13},{6,14},{7,15},{8,16},{9,17... | collective-permute-start | bytes 344072 | tf_op jit(solution)/shard_map/ppermute | solution.py:306
  215.1 23.0 %collective-permute-start.45 = (bf16[16,3584]{1,0:T(8,128)(2,1)S(1)}, bf16[16,3584]{1,0:T(8,128)(2,1)S(1)}, u32[]{:S(2)}, u32[]{:S(2)}) collective-permute-start(bf16[16,3584]{1,0:T(8,128)(2,1)S(1)} %get-tuple-element.192), channel_id=1, source_target_pairs={{0,14},{1,15},{2,8},{3,9},{4,10},{5,11},{6,12},{7,13},{8,22},{9,23... | collective-permute-start | bytes 344072 | tf_op jit(solution)/shard_map/ppermute | solution.py:306
  221.3 17.5 %collective-permute-start.46 = (bf16[16,3584]{1,0:T(8,128)(2,1)S(1)}, bf16[16,3584]{1,0:T(8,128)(2,1)S(1)}, u32[]{:S(2)}, u32[]{:S(2)}) collective-permute-start(bf16[16,3584]{1,0:T(8,128)(2,1)S(1)} %get-tuple-element.193), channel_id=1, source_target_pairs={{0,12},{1,13},{2,14},{3,15},{4,8},{5,9},{6,10},{7,11},{8,20},{9,21... | collective-permute-start | bytes 344072 | tf_op jit(solution)/shard_map/ppermute | solution.py:306
  239.8 24.0 %collective-permute-start.48 = (bf16[16,3584]{1,0:T(8,128)(2,1)S(1)}, bf16[16,3584]{1,0:T(8,128)(2,1)S(1)}, u32[]{:S(2)}, u32[]{:S(2)}) collective-permute-start(bf16[16,3584]{1,0:T(8,128)(2,1)S(1)} %get-tuple-element.196), channel_id=1, source_target_pairs={{8,10},{9,11},{10,12},{11,13},{12,14},{13,15},{14,8},{15,9},{16,18... | collective-permute-start | bytes 344072 | tf_op jit(solution)/shard_map/ppermute | solution.py:306
  240.5 30.3 %collective-permute-start.49 = (bf16[16,3584]{1,0:T(8,128)(2,1)S(1)}, bf16[16,3584]{1,0:T(8,128)(2,1)S(1)}, u32[]{:S(2)}, u32[]{:S(2)}) collective-permute-start(bf16[16,3584]{1,0:T(8,128)(2,1)S(1)} %get-tuple-element.197), channel_id=1, source_target_pairs={{8,12},{9,13},{10,14},{11,15},{12,8},{13,9},{14,10},{15,11},{16,20... | collective-permute-start | bytes 344072 | tf_op jit(solution)/shard_map/ppermute | solution.py:306
  241.2 36.7 %collective-permute-start.50 = (bf16[16,3584]{1,0:T(8,128)(2,1)S(1)}, bf16[16,3584]{1,0:T(8,128)(2,1)S(1)}, u32[]{:S(2)}, u32[]{:S(2)}) collective-permute-start(bf16[16,3584]{1,0:T(8,128)(2,1)S(1)} %get-tuple-element.198), channel_id=1, source_target_pairs={{8,14},{9,15},{10,8},{11,9},{12,10},{13,11},{14,12},{15,13},{16,22... | collective-permute-start | bytes 344072 | tf_op jit(solution)/shard_map/ppermute | solution.py:306
  242.2 49.2 %collective-permute-start.40 = (bf16[16,3584]{1,0:T(8,128)(2,1)S(1)}, bf16[16,3584]{1,0:T(8,128)(2,1)S(1)}, u32[]{:S(2)}, u32[]{:S(2)}) collective-permute-start(bf16[16,3584]{1,0:T(8,128)(2,1)S(1)} %get-tuple-element.183), channel_id=1, source_target_pairs={{24,16},{25,17},{26,18},{27,19},{28,20},{29,21},{30,22},{31,23}} | collective-permute-start | bytes 344072 | tf_op jit(solution)/shard_map/ppermute | solution.py:306
  256.7 41.0 %collective-permute-start.41 = (bf16[16,3584]{1,0:T(8,128)(2,1)S(1)}, bf16[16,3584]{1,0:T(8,128)(2,1)S(1)}, u32[]{:S(2)}, u32[]{:S(2)}) collective-permute-start(bf16[16,3584]{1,0:T(8,128)(2,1)S(1)} %get-tuple-element.184), channel_id=1, source_target_pairs={{24,18},{25,19},{26,20},{27,21},{28,22},{29,23},{30,16},{31,17}} | collective-permute-start | bytes 344072 | tf_op jit(solution)/shard_map/ppermute | solution.py:306
  263.8 40.3 %collective-permute-start.42 = (bf16[16,3584]{1,0:T(8,128)(2,1)S(1)}, bf16[16,3584]{1,0:T(8,128)(2,1)S(1)}, u32[]{:S(2)}, u32[]{:S(2)}) collective-permute-start(bf16[16,3584]{1,0:T(8,128)(2,1)S(1)} %get-tuple-element.185), channel_id=1, source_target_pairs={{24,20},{25,21},{26,22},{27,23},{28,16},{29,17},{30,18},{31,19}} | collective-permute-start | bytes 344072 | tf_op jit(solution)/shard_map/ppermute | solution.py:306
  270.8 39.6 %collective-permute-start.43 = (bf16[16,3584]{1,0:T(8,128)(2,1)S(1)}, bf16[16,3584]{1,0:T(8,128)(2,1)S(1)}, u32[]{:S(2)}, u32[]{:S(2)}) collective-permute-start(bf16[16,3584]{1,0:T(8,128)(2,1)S(1)} %get-tuple-element.186), channel_id=1, source_target_pairs={{24,22},{25,23},{26,16},{27,17},{28,18},{29,19},{30,20},{31,21}} | collective-permute-start | bytes 344072 | tf_op jit(solution)/shard_map/ppermute | solution.py:306
  278.1 33.4 %collective-permute-start.58 = (bf16[16,3584]{1,0:T(8,128)(2,1)S(1)}, bf16[16,3584]{1,0:T(8,128)(2,1)S(1)}, u32[]{:S(2)}, u32[]{:S(2)}) collective-permute-start(bf16[16,3584]{1,0:T(8,128)(2,1)S(1)} %get-tuple-element.216), channel_id=1, source_target_pairs={{8,16},{9,17},{10,18},{11,19},{12,20},{13,21},{14,22},{15,23},{16,... | collective-permute-start | bytes 344072 | tf_op jit(solution)/shard_map/ppermute | solution.py:306
  291.3 39.5 %collective-permute-start.59 = (bf16[16,3584]{1,0:T(8,128)(2,1)S(1)}, bf16[16,3584]{1,0:T(8,128)(2,1)S(1)}, u32[]{:S(2)}, u32[]{:S(2)}) collective-permute-start(bf16[16,3584]{1,0:T(8,128)(2,1)S(1)} %get-tuple-element.217), channel_id=1, source_target_pairs={{8,22},{9,23},{10,16},{11,17},{12,18},{13,19},{14,20},{15,21},{16,... | collective-permute-start | bytes 344072 | tf_op jit(solution)/shard_map/ppermute | solution.py:306
  297.7 40.1 %collective-permute-start.60 = (bf16[16,3584]{1,0:T(8,128)(2,1)S(1)}, bf16[16,3584]{1,0:T(8,128)(2,1)S(1)}, u32[]{:S(2)}, u32[]{:S(2)}) collective-permute-start(bf16[16,3584]{1,0:T(8,128)(2,1)S(1)} %get-tuple-element.218), channel_id=1, source_target_pairs={{8,20},{9,21},{10,22},{11,23},{12,16},{13,17},{14,18},{15,19},{16,... | collective-permute-start | bytes 344072 | tf_op jit(solution)/shard_map/ppermute | solution.py:306
  304.1 33.8 %collective-permute-start.61 = (bf16[16,3584]{1,0:T(8,128)(2,1)S(1)}, bf16[16,3584]{1,0:T(8,128)(2,1)S(1)}, u32[]{:S(2)}, u32[]{:S(2)}) collective-permute-start(bf16[16,3584]{1,0:T(8,128)(2,1)S(1)} %get-tuple-element.219), channel_id=1, source_target_pairs={{8,18},{9,19},{10,20},{11,21},{12,22},{13,23},{14,16},{15,17},{16,... | collective-permute-start | bytes 344072 | tf_op jit(solution)/shard_map/ppermute | solution.py:306
  310.7 41.5 %collective-permute-start.51 = (bf16[16,3584]{1,0:T(8,128)(2,1)S(1)}, bf16[16,3584]{1,0:T(8,128)(2,1)S(1)}, u32[]{:S(2)}, u32[]{:S(2)}) collective-permute-start(bf16[16,3584]{1,0:T(8,128)(2,1)S(1)} %get-tuple-element.204), channel_id=1, source_target_pairs={{16,22},{17,23},{18,16},{19,17},{20,18},{21,19},{22,20},{23,21},{2... | collective-permute-start | bytes 344072 | tf_op jit(solution)/shard_map/ppermute | solution.py:306
  311.5 41.3 %collective-permute-start.52 = (bf16[16,3584]{1,0:T(8,128)(2,1)S(1)}, bf16[16,3584]{1,0:T(8,128)(2,1)S(1)}, u32[]{:S(2)}, u32[]{:S(2)}) collective-permute-start(bf16[16,3584]{1,0:T(8,128)(2,1)S(1)} %get-tuple-element.205), channel_id=1, source_target_pairs={{16,20},{17,21},{18,22},{19,23},{20,16},{21,17},{22,18},{23,19},{2... | collective-permute-start | bytes 344072 | tf_op jit(solution)/shard_map/ppermute | solution.py:306
  330.8 22.0 %collective-permute-start.53 = (bf16[16,3584]{1,0:T(8,128)(2,1)S(1)}, bf16[16,3584]{1,0:T(8,128)(2,1)S(1)}, u32[]{:S(2)}, u32[]{:S(2)}) collective-permute-start(bf16[16,3584]{1,0:T(8,128)(2,1)S(1)} %get-tuple-element.206), channel_id=1, source_target_pairs={{16,18},{17,19},{18,20},{19,21},{20,22},{21,23},{22,16},{23,17},{2... | collective-permute-start | bytes 344072 | tf_op jit(solution)/shard_map/ppermute | solution.py:306
  337.9 32.0 %collective-permute-start.62 = (bf16[16,3584]{1,0:T(8,128)(2,1)S(1)}, bf16[16,3584]{1,0:T(8,128)(2,1)S(1)}, u32[]{:S(2)}, u32[]{:S(2)}) collective-permute-start(bf16[16,3584]{1,0:T(8,128)(2,1)S(1)} %get-tuple-element.221), channel_id=1, source_target_pairs={{16,18},{17,19},{18,20},{19,21},{20,22},{21,23},{22,16},{23,17},{2... | collective-permute-start | bytes 344072 | tf_op jit(solution)/shard_map/ppermute | solution.py:306
  345.1 31.8 %collective-permute-start.63 = (bf16[16,3584]{1,0:T(8,128)(2,1)S(1)}, bf16[16,3584]{1,0:T(8,128)(2,1)S(1)}, u32[]{:S(2)}, u32[]{:S(2)}) collective-permute-start(bf16[16,3584]{1,0:T(8,128)(2,1)S(1)} %get-tuple-element.222), channel_id=1, source_target_pairs={{16,20},{17,21},{18,22},{19,23},{20,16},{21,17},{22,18},{23,19},{2... | collective-permute-start | bytes 344072 | tf_op jit(solution)/shard_map/ppermute | solution.py:306
  352.2 31.8 %collective-permute-start.64 = (bf16[16,3584]{1,0:T(8,128)(2,1)S(1)}, bf16[16,3584]{1,0:T(8,128)(2,1)S(1)}, u32[]{:S(2)}, u32[]{:S(2)}) collective-permute-start(bf16[16,3584]{1,0:T(8,128)(2,1)S(1)} %get-tuple-element.223), channel_id=1, source_target_pairs={{16,22},{17,23},{18,16},{19,17},{20,18},{21,19},{22,20},{23,21},{2... | collective-permute-start | bytes 344072 | tf_op jit(solution)/shard_map/ppermute | solution.py:306
  352.9 31.9 %collective-permute-start.54 = (bf16[16,3584]{1,0:T(8,128)(2,1)S(1)}, bf16[16,3584]{1,0:T(8,128)(2,1)S(1)}, u32[]{:S(2)}, u32[]{:S(2)}) collective-permute-start(bf16[16,3584]{1,0:T(8,128)(2,1)S(1)} %get-tuple-element.208), channel_id=1, source_target_pairs={{16,8},{17,9},{18,10},{19,11},{20,12},{21,13},{22,14},{23,15},{24,... | collective-permute-start | bytes 344072 | tf_op jit(solution)/shard_map/ppermute | solution.py:306
  362.9 36.9 %collective-permute-start.55 = (bf16[16,3584]{1,0:T(8,128)(2,1)S(1)}, bf16[16,3584]{1,0:T(8,128)(2,1)S(1)}, u32[]{:S(2)}, u32[]{:S(2)}) collective-permute-start(bf16[16,3584]{1,0:T(8,128)(2,1)S(1)} %get-tuple-element.209), channel_id=1, source_target_pairs={{16,10},{17,11},{18,12},{19,13},{20,14},{21,15},{22,8},{23,9},{24,... | collective-permute-start | bytes 344072 | tf_op jit(solution)/shard_map/ppermute | solution.py:306
  369.9 36.3 %collective-permute-start.56 = (bf16[16,3584]{1,0:T(8,128)(2,1)S(1)}, bf16[16,3584]{1,0:T(8,128)(2,1)S(1)}, u32[]{:S(2)}, u32[]{:S(2)}) collective-permute-start(bf16[16,3584]{1,0:T(8,128)(2,1)S(1)} %get-tuple-element.210), channel_id=1, source_target_pairs={{16,12},{17,13},{18,14},{19,15},{20,8},{21,9},{22,10},{23,11},{24,... | collective-permute-start | bytes 344072 | tf_op jit(solution)/shard_map/ppermute | solution.py:306
  376.9 35.6 %collective-permute-start.57 = (bf16[16,3584]{1,0:T(8,128)(2,1)S(1)}, bf16[16,3584]{1,0:T(8,128)(2,1)S(1)}, u32[]{:S(2)}, u32[]{:S(2)}) collective-permute-start(bf16[16,3584]{1,0:T(8,128)(2,1)S(1)} %get-tuple-element.211), channel_id=1, source_target_pairs={{16,14},{17,15},{18,8},{19,9},{20,10},{21,11},{22,12},{23,13},{24,... | collective-permute-start | bytes 344072 | tf_op jit(solution)/shard_map/ppermute | solution.py:306
  384.1 29.8 %collective-permute-start.72 = (bf16[16,3584]{1,0:T(8,128)(2,1)S(1)}, bf16[16,3584]{1,0:T(8,128)(2,1)S(1)}, u32[]{:S(2)}, u32[]{:S(2)}) collective-permute-start(bf16[16,3584]{1,0:T(8,128)(2,1)S(1)} %get-tuple-element.241), channel_id=1, source_target_pairs={{16,24},{17,25},{18,26},{19,27},{20,28},{21,29},{22,30},{23,31}} | collective-permute-start | bytes 344072 | tf_op jit(solution)/shard_map/ppermute | solution.py:306
  384.8 29.9 %collective-permute-start.73 = (bf16[16,3584]{1,0:T(8,128)(2,1)S(1)}, bf16[16,3584]{1,0:T(8,128)(2,1)S(1)}, u32[]{:S(2)}, u32[]{:S(2)}) collective-permute-start(bf16[16,3584]{1,0:T(8,128)(2,1)S(1)} %get-tuple-element.242), channel_id=1, source_target_pairs={{16,30},{17,31},{18,24},{19,25},{20,26},{21,27},{22,28},{23,29}} | collective-permute-start | bytes 344072 | tf_op jit(solution)/shard_map/ppermute | solution.py:306
  399.8 15.7 %collective-permute-start.74 = (bf16[16,3584]{1,0:T(8,128)(2,1)S(1)}, bf16[16,3584]{1,0:T(8,128)(2,1)S(1)}, u32[]{:S(2)}, u32[]{:S(2)}) collective-permute-start(bf16[16,3584]{1,0:T(8,128)(2,1)S(1)} %get-tuple-element.243), channel_id=1, source_target_pairs={{16,28},{17,29},{18,30},{19,31},{20,24},{21,25},{22,26},{23,27}} | collective-permute-start | bytes 344072 | tf_op jit(solution)/shard_map/ppermute | solution.py:306
  417.6 32.5 %collective-permute-start.68 = (bf16[16,3584]{1,0:T(8,128)(2,1)S(1)}, bf16[16,3584]{1,0:T(8,128)(2,1)S(1)}, u32[]{:S(2)}, u32[]{:S(2)}) collective-permute-start(bf16[16,3584]{1,0:T(8,128)(2,1)S(1)} %get-tuple-element.233), channel_id=1, source_target_pairs={{8,0},{9,1},{10,2},{11,3},{12,4},{13,5},{14,6},{15,7},{16,8},{17,9... | collective-permute-start | bytes 344072 | tf_op jit(solution)/shard_map/ppermute | solution.py:306
  418.9 35.4 %collective-permute-start.69 = (bf16[16,3584]{1,0:T(8,128)(2,1)S(1)}, bf16[16,3584]{1,0:T(8,128)(2,1)S(1)}, u32[]{:S(2)}, u32[]{:S(2)}) collective-permute-start(bf16[16,3584]{1,0:T(8,128)(2,1)S(1)} %get-tuple-element.234), channel_id=1, source_target_pairs={{8,2},{9,3},{10,4},{11,5},{12,6},{13,7},{14,0},{15,1},{16,10},{17,... | collective-permute-start | bytes 344072 | tf_op jit(solution)/shard_map/ppermute | solution.py:306
  420.2 38.3 %collective-permute-start.70 = (bf16[16,3584]{1,0:T(8,128)(2,1)S(1)}, bf16[16,3584]{1,0:T(8,128)(2,1)S(1)}, u32[]{:S(2)}, u32[]{:S(2)}) collective-permute-start(bf16[16,3584]{1,0:T(8,128)(2,1)S(1)} %get-tuple-element.235), channel_id=1, source_target_pairs={{8,4},{9,5},{10,6},{11,7},{12,0},{13,1},{14,2},{15,3},{16,12},{17,... | collective-permute-start | bytes 344072 | tf_op jit(solution)/shard_map/ppermute | solution.py:306
  421.6 37.3 %collective-permute-start.71 = (bf16[16,3584]{1,0:T(8,128)(2,1)S(1)}, bf16[16,3584]{1,0:T(8,128)(2,1)S(1)}, u32[]{:S(2)}, u32[]{:S(2)}) collective-permute-start(bf16[16,3584]{1,0:T(8,128)(2,1)S(1)} %get-tuple-element.236), channel_id=1, source_target_pairs={{8,6},{9,7},{10,0},{11,1},{12,2},{13,3},{14,4},{15,5},{16,14},{17,... | collective-permute-start | bytes 344072 | tf_op jit(solution)/shard_map/ppermute | solution.py:306
  544.6 27.5 %collective-permute-start.89 = (bf16[16,3584]{1,0:T(8,128)(2,1)S(1)}, bf16[16,3584]{1,0:T(8,128)(2,1)S(1)}, u32[]{:S(2)}, u32[]{:S(2)}) collective-permute-start(bf16[16,3584]{1,0:T(8,128)(2,1)S(1)} %get-tuple-element.267), channel_id=1, source_target_pairs={{8,0},{9,1},{10,2},{11,3},{12,4},{13,5},{14,6},{15,7},{16,8},{17,9... | collective-permute-start | bytes 344072 | tf_op jit(solution)/shard_map/ppermute | solution.py:306
  552.8 19.4 %collective-permute-start.90 = (bf16[16,3584]{1,0:T(8,128)(2,1)S(1)}, bf16[16,3584]{1,0:T(8,128)(2,1)S(1)}, u32[]{:S(2)}, u32[]{:S(2)}) collective-permute-start(bf16[16,3584]{1,0:T(8,128)(2,1)S(1)} %get-tuple-element.268), channel_id=1, source_target_pairs={{8,2},{9,3},{10,4},{11,5},{12,6},{13,7},{14,0},{15,1},{16,10},{17,... | collective-permute-start | bytes 344072 | tf_op jit(solution)/shard_map/ppermute | solution.py:306
  559.2 16.6 %collective-permute-start.91 = (bf16[16,3584]{1,0:T(8,128)(2,1)S(1)}, bf16[16,3584]{1,0:T(8,128)(2,1)S(1)}, u32[]{:S(2)}, u32[]{:S(2)}) collective-permute-start(bf16[16,3584]{1,0:T(8,128)(2,1)S(1)} %get-tuple-element.269), channel_id=1, source_target_pairs={{8,4},{9,5},{10,6},{11,7},{12,0},{13,1},{14,2},{15,3},{16,12},{17,... | collective-permute-start | bytes 344072 | tf_op jit(solution)/shard_map/ppermute | solution.py:306
  (153 other events, 5144.5 us)

commit v2 on v1

--- a/solution.py
+++ b/solution.py
@@ -13,7 +13,8 @@
 
 in_vmem = pl.BlockSpec(memory_space=pltpu.VMEM)
 in_smem = pl.BlockSpec(memory_space=pltpu.SMEM)
-anywhere = pl.BlockSpec(memory_space=pl.ANY)
+in_hbm = pl.BlockSpec(memory_space=pltpu.HBM)
+lanes = 128
 
 
 def spans(total, size):
@@ -31,6 +32,19 @@
 
 def product_t(left, right):
     return lax.dot_general(left, right, last_with_last, preferred_element_type=jnp.float32)
+
+
+def coded(column):
+    high = column.astype(jnp.bfloat16).astype(jnp.float32)
+    left = column - high
+    middle = left.astype(jnp.bfloat16).astype(jnp.float32)
+    lane = lax.broadcasted_iota(jnp.int32, (column.shape[0], lanes), 1)
+    spread = jnp.where(lane == 1, middle, jnp.where(lane == 2, left - middle, 0.0))
+    return jnp.where(lane == 0, high, spread).astype(jnp.bfloat16)
+
+
+def decoded(columns):
+    return jnp.sum(columns.astype(jnp.float32), axis=-1, keepdims=True)
 
 
 def weight_copies(half_refs, buffers, sems):
@@ -44,9 +58,9 @@
 
 
 def forward_kernel(slot, micro_count, parts, *refs):
-    sec_ref, gain_ref, route_ref = refs[:3]
-    x_refs = refs[3 : 3 + parts]
-    rest = refs[3 + parts :]
+    sec_ref, gain_ref = refs[:2]
+    x_refs = refs[2 : 2 + parts]
+    rest = refs[2 + parts :]
     half_refs = [rest[0:3], rest[3:6]]
     out_refs = rest[6 : 6 + parts]
     save_x, save_gate, save_up, save_rows = rest[6 + parts : 10 + parts]
@@ -65,12 +79,11 @@
         for half in range(2):
             copies[2][half].start()
         for part in range(parts):
-            block = x_refs[part][...]
-            values = block.astype(jnp.float32)
+            values = x_refs[part][:, :width].astype(jnp.float32)
             inv_rms = lax.rsqrt(jnp.mean(values * values, axis=-1, keepdims=True) + epsilon)
             here = pl.ds(part * rows, rows)
             normed[here, :] = (values * inv_rms * gain_ref[...]).astype(jnp.bfloat16)
-            save_x[here, :] = block
+            save_x[here, :] = x_refs[part][...]
         for half in range(2):
             side = pl.ds(half * hidden_dim, hidden_dim)
             copies[0][half].wait()
@@ -82,22 +95,21 @@
             hidden[half] = (gate_pre * jax.nn.sigmoid(gate_pre) * up_pre).astype(jnp.bfloat16)
         copies[2][0].wait()
         copies[2][1].wait()
-        route = route_ref[micro]
+        route = [decoded(x_refs[part][:, width:]) for part in range(parts)]
         for span in spans(width, 256):
             made = product(hidden[0], down_buf[0, :, span])
             made = made + product(hidden[1], down_buf[1, :, span])
             save_rows[:, span] = made
-            added = route * made
             for part in range(parts):
-                here = slice(part * rows, (part + 1) * rows)
+                added = route[part] * made[part * rows : (part + 1) * rows]
                 values = x_refs[part][:, span].astype(jnp.float32)
-                out_refs[part][:, span] = (values + added[here]).astype(jnp.bfloat16)
+                out_refs[part][:, span] = (values + added).astype(jnp.bfloat16)
 
 
 def backward_kernel(slot, counts, candidates, parts, *refs):
     section_count, micro_count = counts
-    sec_ref, gain_ref, route_ref = refs[:3]
-    rest = refs[3:]
+    sec_ref, gain_ref = refs[:2]
+    rest = refs[2:]
     arrived = rest[:parts]
     first = rest[parts : 2 * parts]
     rest = rest[2 * parts :]
@@ -108,9 +120,8 @@
         saved[section] = rest[:4]
         rest = rest[4:]
     out_refs = rest[:parts]
-    gate_out = rest[parts]
     (gate_buf, up_buf, down_buf, grad_buf, x_buf, pre_gate, pre_up, rows_buf, grad_rows, scaled_buf,
-     sems, state_sems, grad_sems) = rest[parts + 1 :]
+     sems, state_sems, grad_sems) = rest[parts:]
     sec = sec_ref[0]
     micro = slot - 2 * (section_count - 1) + sec
     width = gain_ref.shape[1]
@@ -147,7 +158,7 @@
             copies[1][half].start()
         for section in candidates:
             for_section(section, lambda copy: copy.wait())
-        route = route_ref[micro]
+        route = decoded(x_buf[:, width:])
         gate_grad = jnp.zeros((slots, 1), jnp.float32)
         square = jnp.zeros((slots, 1), jnp.float32)
         for span in spans(width, 512):
@@ -156,13 +167,15 @@
             grad_rows[:, span] = (route * grad_f).astype(jnp.bfloat16)
             values = x_buf[:, span].astype(jnp.float32)
             square += jnp.sum(values * values, axis=-1, keepdims=True)
-        gate_out[...] = jnp.broadcast_to(gate_grad, gate_out.shape)
+        gate_columns = coded(gate_grad)
+        for part in range(parts):
+            out_refs[part][:, width:] = gate_columns[part * rows : (part + 1) * rows]
         inv_rms = lax.rsqrt(square / width + epsilon)
         grads = []
         for half in range(2):
             side = pl.ds(half * hidden_dim, hidden_dim)
             copies[2][half].wait()
-            grad_hidden = product_t(grad_rows[...], down_buf[half])
+            grad_hidden = product_t(down_buf[half], grad_rows[...]).T
             gate_pre = pre_gate[:, side]
             sigma = jax.nn.sigmoid(gate_pre)
             grad_gate = grad_hidden * pre_up[:, side] * sigma * (1.0 + gate_pre * (1.0 - sigma))
@@ -173,11 +186,11 @@
             copies[1][half].wait()
         dotted = jnp.zeros((slots, 1), jnp.float32)
         for span in spans(width, 256):
-            total = product_t(grads[0][0], gate_buf[0, span, :])
-            total = total + product_t(grads[0][1], up_buf[0, span, :])
-            total = total + product_t(grads[1][0], gate_buf[1, span, :])
-            total = total + product_t(grads[1][1], up_buf[1, span, :])
-            scaled = total * gain_ref[:, span]
+            total = product_t(gate_buf[0, span, :], grads[0][0])
+            total = total + product_t(up_buf[0, span, :], grads[0][1])
+            total = total + product_t(gate_buf[1, span, :], grads[1][0])
+            total = total + product_t(up_buf[1, span, :], grads[1][1])
+            scaled = total.T * gain_ref[:, span]
             scaled_buf[:, span] = scaled
             dotted += jnp.sum(x_buf[:, span].astype(jnp.float32) * scaled, axis=-1, keepdims=True)
         back = inv_rms * inv_rms * inv_rms * (dotted / width)
@@ -192,8 +205,8 @@
 
 
 def forward_router(slot, micro_count, parts, has_first, has_rest, *refs):
-    sec_ref, place_ref, move_ref = refs[:3]
-    rest = refs[3:]
+    sec_ref, route_ref, place_ref, move_ref = refs[:4]
+    rest = refs[4:]
     tokens_ref = rest[0] if has_first else None
     rest = rest[1:] if has_first else rest
     arrived = rest[:parts] if has_rest else None
@@ -201,10 +214,13 @@
     out_refs = rest[:parts]
     sec = sec_ref[0]
     micro = slot - sec
-    width = out_refs[0].shape[1]
+    width = out_refs[0].shape[1] - lanes
     rows = out_refs[0].shape[0]
 
-    def put(table, source):
+    def put(number, table, source):
+        columns = coded(route_ref[number])
+        for part in range(parts):
+            out_refs[part][:, width:] = columns[part * rows : (part + 1) * rows]
         for span in spans(width, 512):
             made = product(table, source(span)).astype(jnp.bfloat16)
             for part in range(parts):
@@ -214,13 +230,14 @@
 
         @pl.when(sec == 0)
         def _():
-            put(place_ref[slot], lambda span: tokens_ref[:, span])
+            put(slot, place_ref[slot], lambda span: tokens_ref[:, span])
 
     if has_rest:
 
         @pl.when((sec > 0) & (micro >= 0) & (micro < micro_count))
         def _():
             put(
+                micro,
                 move_ref[micro],
                 lambda span: jnp.concatenate([ref[:, span] for ref in arrived], axis=0),
             )
@@ -230,13 +247,13 @@
     section_count, micro_count = counts
     sec_ref, take_ref, move_ref = refs[:3]
     arrived = refs[3 : 3 + parts]
-    rest = refs[3 + parts + (1 if has_former else 0) :]
-    result = rest[0]
-    out_refs = rest[1 : 1 + parts] if onward else []
-    ordered, sem = rest[1 + len(out_refs) :]
+    rest = refs[3 + parts + (2 if has_former else 0) :]
+    result, gates = rest[:2]
+    out_refs = rest[2 : 2 + parts] if onward else []
+    ordered, gate_rows, sems = rest[2 + len(out_refs) :]
     sec = sec_ref[0]
     micro = slot - 2 * (section_count - 1) + sec
-    width = arrived[0].shape[1]
+    width = arrived[0].shape[1] - lanes
     rows = arrived[0].shape[0]
 
     @pl.when((micro >= 0) & (micro < micro_count))
@@ -255,9 +272,14 @@
 
         for span in spans(width, 512):
             ordered[:, span] = product(take_ref[micro], source(span)).astype(jnp.bfloat16)
-        copy = pltpu.make_async_copy(ordered, result.at[micro], sem)
+        copy = pltpu.make_async_copy(ordered, result.at[micro], sems.at[0])
         copy.start()
+        columns = decoded(product(take_ref[micro], source(pl.ds(width, lanes))))
+        gate_rows[...] = jnp.broadcast_to(columns, gate_rows.shape)
+        gate_copy = pltpu.make_async_copy(gate_rows, gates.at[micro], sems.at[1])
+        gate_copy.start()
         copy.wait()
+        gate_copy.wait()
 
 
 def slots_of(route_ids, expert_count, capacity, turn):
@@ -328,7 +350,12 @@
     sec = section.reshape(1).astype(jnp.int32)
     gain = norm_gain
     ids = expert_ids[0, :, :, 0]
-    former_ids = lax.ppermute(ids, "section", [(s, s + 1) for s in sections[:-1]])
+    onto_next = [(s, s + 1) for s in sections[:-1]]
+    onto_former = [(s + 1, s) for s in sections[:-1]]
+    within = [(s, s) for s in sections]
+    former_ids = lax.ppermute(
+        ids, both, [(a * device_count + i, b * device_count + i) for a, b in onto_next for i in range(device_count)]
+    )
     slot_own = slots_of(ids, expert_count, capacity, turn)
     slot_former = slots_of(former_ids, expert_count, capacity, turn)
     numbers = jnp.arange(slots, dtype=jnp.int32)
@@ -339,8 +366,7 @@
     move_forward = jnp.einsum("mjt,mit->mji", place_own, place_former)
     move_back = jnp.einsum("mjt,mit->mji", place_former, place_own)
     route_slots = jnp.sum(jnp.where(is_own, gate_weights[0, :, None, :, 0], 0.0), axis=-1)
-    route_parts = exchange(cut(route_slots[:, :, None]), [(s, s) for s in sections], 1)
-    route = jnp.concatenate(route_parts, axis=1)
+    route = route_slots[:, :, None]
 
     tokens_all = [tokens_in[0]]
     cotangent_all = []
@@ -356,6 +382,7 @@
     first_grads = exchange(cut(packed), [(first_back, first_back)], 1)
 
     chunk = jax.ShapeDtypeStruct((rows, model_dim), jnp.bfloat16)
+    wide = jax.ShapeDtypeStruct((rows, model_dim + lanes), jnp.bfloat16)
     weight_scratch = [
         pltpu.VMEM((2, model_dim, hidden_dim), jnp.bfloat16),
         pltpu.VMEM((2, model_dim, hidden_dim), jnp.bfloat16),
@@ -365,7 +392,7 @@
     flops = 2 * slots * 6 * model_dim * hidden_dim
     heavy = pl.CostEstimate(flops=flops, bytes_accessed=weight_bytes, transcendentals=0)
     state_shapes = [
-        jax.ShapeDtypeStruct((slots, model_dim), jnp.bfloat16),
+        jax.ShapeDtypeStruct((slots, model_dim + lanes), jnp.bfloat16),
         jax.ShapeDtypeStruct((slots, 2 * hidden_dim), jnp.float32),
         jax.ShapeDtypeStruct((slots, 2 * hidden_dim), jnp.float32),
         jax.ShapeDtypeStruct((slots, model_dim), jnp.float32),
@@ -374,8 +401,7 @@
     saved = {}
     ahead = None
     behind = None
-    gate_slots = []
-    result = None
+    results = None
     for slot in range(slot_count):
         forward_on = [s for s in sections if 0 <= slot - s < micro_count]
         if forward_on:
@@ -383,24 +409,25 @@
             has_rest = ahead is not None
             packed = pl.pallas_call(
                 partial(forward_router, slot, micro_count, parts, has_first, has_rest),
-                out_shape=[chunk] * parts,
-                in_specs=[in_smem, in_vmem, in_vmem]
+                out_shape=[wide] * parts,
+                in_specs=[in_smem, in_vmem, in_vmem, in_vmem]
                 + [in_vmem] * ((1 if has_first else 0) + (parts if has_rest else 0)),
                 out_specs=[in_vmem] * parts,
                 compiler_params=params(16),
                 name=f"route_forward_{slot}",
             )(
                 sec,
+                route,
                 place_own,
                 move_forward,
                 *([tokens_all[slot]] if has_first else []),
                 *(ahead if has_rest else []),
             )
-            moved = exchange(packed, [(s, s) for s in forward_on], 1)
+            moved = exchange(packed, within, 1)
             outs = pl.pallas_call(
                 partial(forward_kernel, slot, micro_count, parts),
                 out_shape=[chunk] * parts + state_shapes,
-                in_specs=[in_smem, in_vmem, in_vmem] + [in_vmem] * parts + [anywhere] * 6,
+                in_specs=[in_smem, in_vmem] + [in_vmem] * parts + [in_hbm] * 6,
                 out_specs=[in_vmem] * (parts + 4),
                 scratch_shapes=weight_scratch
                 + [
@@ -411,28 +438,30 @@
                 compiler_params=params(40),
                 cost_estimate=heavy,
                 name=f"expert_forward_{slot}",
-            )(sec, gain, route, *moved, *weights)
+            )(sec, gain, *moved, *weights)
             x_rows, pre_gate, pre_up, made = outs[parts:]
             saved[slot] = (made, x_rows, pre_gate, pre_up)
-            jobs = [(s, s + 1) for s in forward_on if s + 1 < section_count]
-            ahead = exchange(outs[:parts], jobs, -1) if jobs else None
+            more = any(s + 1 < section_count for s in forward_on)
+            ahead = exchange(outs[:parts], onto_next, -1) if more else None
         backward_on = [s for s in sections if 0 <= slot - 2 * first_back + s < micro_count]
         if backward_on:
-            jobs = [(s + 1, s) for s in backward_on if s < first_back]
-            grads = exchange(behind, jobs, 1) if jobs else [part[0] for part in first_grads]
+            if behind is None:
+                grads = [part[0] for part in first_grads]
+            else:
+                grads = exchange(behind, onto_former, 1)
             states = []
             for s in backward_on:
                 states += list(saved[slot - 2 * first_back + 2 * s])
             outs = pl.pallas_call(
                 partial(backward_kernel, slot, counts, backward_on, parts),
-                out_shape=[chunk] * parts + [jax.ShapeDtypeStruct((slots, 128), jnp.float32)],
-                in_specs=[in_smem, in_vmem, in_vmem]
-                + [anywhere] * (2 * parts + 6 + len(states)),
-                out_specs=[in_vmem] * (parts + 1),
+                out_shape=[wide] * parts,
+                in_specs=[in_smem, in_vmem] + [pl.BlockSpec(memory_space=pl.ANY)] * (2 * parts)
+                + [in_hbm] * (6 + len(states)),
+                out_specs=[in_vmem] * parts,
                 scratch_shapes=weight_scratch
                 + [
                     pltpu.VMEM((slots, model_dim), jnp.bfloat16),
-                    pltpu.VMEM((slots, model_dim), jnp.bfloat16),
+                    pltpu.VMEM((slots, model_dim + lanes), jnp.bfloat16),
                     pltpu.VMEM((slots, 2 * hidden_dim), jnp.float32),
                     pltpu.VMEM((slots, 2 * hidden_dim), jnp.float32),
                     pltpu.VMEM((slots, model_dim), jnp.float32),
@@ -445,35 +474,34 @@
                 compiler_params=params(40),
                 cost_estimate=heavy,
                 name=f"expert_backward_{slot}",
-            )(sec, gain, route, *grads, *first_grads, *weights, *states)
-            gate_slots.append(outs[parts][:, 0])
-            home = exchange(outs[:parts], [(s, s) for s in backward_on], -1)
+            )(sec, gain, *grads, *first_grads, *weights, *states)
+            home = exchange(outs, within, -1)
             onward = slot + 1 < slot_count
-            has_former = result is not None
+            has_former = results is not None
             outs = pl.pallas_call(
                 partial(backward_router, slot, counts, parts, has_former, onward),
-                out_shape=[jax.ShapeDtypeStruct((micro_count, tok_rows, model_dim), jnp.bfloat16)]
+                out_shape=[
+                    jax.ShapeDtypeStruct((micro_count, tok_rows, model_dim), jnp.bfloat16),
+                    jax.ShapeDtypeStruct((micro_count, tok_rows, lanes), jnp.float32),
+                ]
                 + [chunk] * (parts if onward else 0),
                 in_specs=[in_smem, in_vmem, in_vmem]
                 + [in_vmem] * parts
-                + [anywhere] * (1 if has_former else 0),
-                out_specs=[anywhere] + [in_vmem] * (parts if onward else 0),
+                + [in_hbm] * (2 if has_former else 0),
+                out_specs=[in_hbm] * 2 + [in_vmem] * (parts if onward else 0),
                 scratch_shapes=[
                     pltpu.VMEM((tok_rows, model_dim), jnp.bfloat16),
-                    pltpu.SemaphoreType.DMA,
+                    pltpu.VMEM((tok_rows, lanes), jnp.float32),
+                    pltpu.SemaphoreType.DMA((2,)),
                 ],
-                input_output_aliases={3 + parts: 0} if has_former else {},
+                input_output_aliases={3 + parts: 0, 4 + parts: 1} if has_former else {},
                 compiler_params=params(16),
                 name=f"route_backward_{slot}",
-            )(sec, take_own, move_back, *home, *([result] if has_former else []))
-            result = outs[0]
-            behind = outs[1:]
-
-    gates = lax.dynamic_slice_in_dim(jnp.stack(gate_slots), first_back - section, micro_count, 0)
-    gate_parts = exchange(cut(gates[:, :, None]), [(s, s) for s in sections], -1)
-    gates = jnp.concatenate(gate_parts, axis=1)
-    gate_out = jnp.sum(jnp.where(is_own, gates, 0.0), axis=1)
-    return (result[None], gate_out[None, :, :, None])
+            )(sec, take_own, move_back, *home, *(results if has_former else []))
+            results = outs[:2]
+            behind = outs[2:]
+
+    return (results[0][None], results[1][None, :, :, :1])
 
 
 def solution(mesh):

time: 682 us -> 482 us (0.71)
  starting transfers between devices: 421 us -> 239 us
  local copies, waits for them, and re-layouts: 37.9 us -> 22.4 us
    ppermute x99 -> x93, starting transfers between devices: 383 us -> 229 us  [exchange(): moved[step] = lax.ppermute(chunks[step], both, pairs)]
    ppermute x3, starting transfers between devices: 18.6 us -> 1.03 us  [body(): other = tuple((lax.ppermute(matrix, 'expert', swap) for matrix in own))]
    unnamed x190 -> x142, local copies, waits for them, and re-layouts: 36.7 us -> 21.4 us
    ppermute x3, starting transfers between devices: 15.5 us -> 4.72 us  [body(): lax.ppermute(sent, 'section', [(step, 0), (step - 1, section_count - 1)])]
    ppermute x99 -> x93, waiting for transfers between devices: 120 us -> 115 us  [exchange(): moved[step] = lax.ppermute(chunks[step], both, pairs)]
  transfers between devices with their start and end apart: 106 -> 100, of which waited for: 35 -> 45; matrix products, arithmetic and copies ran while one was open for 1% -> 1% of each run, Pallas kernels for 3% -> 5%
where the time goes in v2:
time: 482 us; the launch traced here: 473 us
  starting transfers between devices  239 us (50%)
  waiting for transfers between devices  116 us (24%)
  Pallas kernels  87.2 us (18%)
  local copies, waits for them, and re-layouts  22.4 us (5%)
  other arithmetic  4.84 us (1%)
    ppermute x93, starting transfers between devices, exchange(): moved[step] = lax.ppermute(chunks[step], both, pairs)  229 us
    ppermute x93, waiting for transfers between devices, exchange(): moved[step] = lax.ppermute(chunks[step], both, pairs)  115 us
    pallas_call x7, Pallas kernels, body(): pl.pallas_call(partial(backward_kernel, slot, counts, backward_on, parts)...  55.9 us
    pallas_call x7, Pallas kernels, body(): pl.pallas_call(partial(forward_kernel, slot, micro_count, parts), out_sha...  26.2 us
    unnamed x142, local copies, waits for them, and re-layouts  21.4 us
  transfers between devices with their start and end apart: 100, of which 45 were waited for; matrix products, arithmetic and copies ran while one was open for 1% of the time, Pallas kernels for 5%

profile of v2, /device:TPU:0, one launch (start us, length us, event | category | flops | bytes accessed | tf_op | source)
XLA Modules:
  0.0 473.0 jit_solution(3518662304072974363)
XLA Ops:
  1.7 4.5 collective-permute-start
  15.7 3.8 collective-permute-done.10.refs_3_
  35.5 6.4 %expert_forward_0.1 = (bf16[16,3584]{1,0:T(8,128)(2,1)S(1)}, bf16[16,3584]{1,0:T(8,128)(2,1)S(1)}, bf16[16,3584]{1,0:T(8,128)(2,1)S(1)}, bf16[16,3584]{1,0:T(8,1...) custom-call(s32[1]{0:T(128)} %bitcast.refs_0_, ...), custom_call_target="tpu_custom_call" | custom-call | flops 1409286144 | bytes 22020096 | tf_op jit(solution)/shard_map/expert_forward_0/pallas_call | solution.py:427
  43.3 3.8 collective-permute-start.14
  48.6 3.8 collective-permute-start.16
  63.5 3.3 collective-permute-done.18.refs_4_
  66.8 6.2 %expert_forward_1.1 = (bf16[16,3584]{1,0:T(8,128)(2,1)S(1)}, bf16[16,3584]{1,0:T(8,128)(2,1)S(1)}, bf16[16,3584]{1,0:T(8,128)(2,1)S(1)}, bf16[16,3584]{1,0:T(8,1...) custom-call(s32[1]{0:T(128)} %bitcast.refs_0_, ...), custom_call_target="tpu_custom_call" | custom-call | flops 1409286144 | bytes 22020096 | tf_op jit(solution)/shard_map/expert_forward_1/pallas_call | solution.py:427
  73.1 5.0 %collective-permute-start.20 = (bf16[16,3584]{1,0:T(8,128)(2,1)S(1)}, bf16[16,3584]{1,0:T(8,128)(2,1)S(1)}, u32[]{:S(2)}, u32[]{:S(2)}) collective-permute-start(bf16[16,3584]{1,0:T(8,128)(2,1)S(1)} %get-tuple-element.160), channel_id=1, source_target_pairs={{0,8},{1,9},{2,10},{3,11},{4,12},{5,13},{6,14},{7,15},{8,16},{9,17... | collective-permute-start | bytes 344072 | tf_op jit(solution)/shard_map/ppermute | solution.py:328
  78.1 3.8 collective-permute-start.21
  82.0 9.6 %collective-permute-start.22 = (bf16[16,3584]{1,0:T(8,128)(2,1)S(1)}, bf16[16,3584]{1,0:T(8,128)(2,1)S(1)}, u32[]{:S(2)}, u32[]{:S(2)}) collective-permute-start(bf16[16,3584]{1,0:T(8,128)(2,1)S(1)} %get-tuple-element.162), channel_id=1, source_target_pairs={{0,12},{1,13},{2,14},{3,15},{4,8},{5,9},{6,10},{7,11},{8,20},{9,21... | collective-permute-start | bytes 344072 | tf_op jit(solution)/shard_map/ppermute | solution.py:328
  91.5 3.8 collective-permute-start.23
  108.2 6.4 %expert_forward_2.1 = (bf16[16,3584]{1,0:T(8,128)(2,1)S(1)}, bf16[16,3584]{1,0:T(8,128)(2,1)S(1)}, bf16[16,3584]{1,0:T(8,128)(2,1)S(1)}, bf16[16,3584]{1,0:T(8,1...) custom-call(s32[1]{0:T(128)} %bitcast.refs_0_, ...), custom_call_target="tpu_custom_call" | custom-call | flops 1409286144 | bytes 22020096 | tf_op jit(solution)/shard_map/expert_forward_2/pallas_call | solution.py:427
  114.6 6.0 %collective-permute-start.27 = (bf16[16,3584]{1,0:T(8,128)(2,1)S(1)}, bf16[16,3584]{1,0:T(8,128)(2,1)S(1)}, u32[]{:S(2)}, u32[]{:S(2)}) collective-permute-start(bf16[16,3584]{1,0:T(8,128)(2,1)S(1)} %get-tuple-element.168), channel_id=1, source_target_pairs={{0,8},{1,9},{2,10},{3,11},{4,12},{5,13},{6,14},{7,15},{8,16},{9,17... | collective-permute-start | bytes 344072 | tf_op jit(solution)/shard_map/ppermute | solution.py:328
  120.6 6.9 %collective-permute-start.28 = (bf16[16,3584]{1,0:T(8,128)(2,1)S(1)}, bf16[16,3584]{1,0:T(8,128)(2,1)S(1)}, u32[]{:S(2)}, u32[]{:S(2)}) collective-permute-start(bf16[16,3584]{1,0:T(8,128)(2,1)S(1)} %get-tuple-element.169), channel_id=1, source_target_pairs={{0,14},{1,15},{2,8},{3,9},{4,10},{5,11},{6,12},{7,13},{8,22},{9,23... | collective-permute-start | bytes 344072 | tf_op jit(solution)/shard_map/ppermute | solution.py:328
  127.5 4.4 collective-permute-start.29
  135.3 3.4 collective-permute-done.30.refs_8_
  138.9 3.5 collective-permute-start.31
  145.6 3.4 collective-permute-done.32.refs_4_
  149.1 6.2 %expert_forward_3.1 = (bf16[16,3584]{1,0:T(8,128)(2,1)S(1)}, bf16[16,3584]{1,0:T(8,128)(2,1)S(1)}, bf16[16,3584]{1,0:T(8,128)(2,1)S(1)}, bf16[16,3584]{1,0:T(8,1...) custom-call(s32[1]{0:T(128)} %bitcast.refs_0_, ...), custom_call_target="tpu_custom_call" | custom-call | flops 1409286144 | bytes 22020096 | tf_op jit(solution)/shard_map/expert_forward_3/pallas_call | solution.py:427
  155.3 5.2 %collective-permute-start.41 = (bf16[16,3584]{1,0:T(8,128)(2,1)S(1)}, bf16[16,3584]{1,0:T(8,128)(2,1)S(1)}, u32[]{:S(2)}, u32[]{:S(2)}) collective-permute-start(bf16[16,3584]{1,0:T(8,128)(2,1)S(1)} %get-tuple-element.192), channel_id=1, source_target_pairs={{0,8},{1,9},{2,10},{3,11},{4,12},{5,13},{6,14},{7,15},{8,16},{9,17... | collective-permute-start | bytes 344072 | tf_op jit(solution)/shard_map/ppermute | solution.py:328
  160.5 4.4 collective-permute-start.42
  173.4 7.1 %collective-permute-start.45 = (bf16[16,3712]{1,0:T(8,128)(2,1)S(1)}, bf16[16,3712]{1,0:T(8,128)(2,1)S(1)}, u32[]{:S(2)}, u32[]{:S(2)}) collective-permute-start(bf16[16,3712]{1,0:T(8,128)(2,1)S(1)} %get-tuple-element.197), channel_id=1, source_target_pairs={{0,2},{1,3},{2,4},{3,5},{4,6},{5,7},{6,0},{7,1},{8,10},{9,11},{10,... | collective-permute-start | bytes 356360 | tf_op jit(solution)/shard_map/ppermute | solution.py:328
  193.5 3.9 collective-permute-done.38.refs_3_
  203.7 5.8 %collective-permute-start.55 = (bf16[16,3584]{1,0:T(8,128)(2,1)S(1)}, bf16[16,3584]{1,0:T(8,128)(2,1)S(1)}, u32[]{:S(2)}, u32[]{:S(2)}) collective-permute-start(bf16[16,3584]{1,0:T(8,128)(2,1)S(1)} %get-tuple-element.218), channel_id=1, source_target_pairs={{0,8},{1,9},{2,10},{3,11},{4,12},{5,13},{6,14},{7,15},{8,16},{9,17... | collective-permute-start | bytes 344072 | tf_op jit(solution)/shard_map/ppermute | solution.py:328
  209.4 16.5 %collective-permute-start.56 = (bf16[16,3584]{1,0:T(8,128)(2,1)S(1)}, bf16[16,3584]{1,0:T(8,128)(2,1)S(1)}, u32[]{:S(2)}, u32[]{:S(2)}) collective-permute-start(bf16[16,3584]{1,0:T(8,128)(2,1)S(1)} %get-tuple-element.219), channel_id=1, source_target_pairs={{0,14},{1,15},{2,8},{3,9},{4,10},{5,11},{6,12},{7,13},{8,22},{9,23... | collective-permute-start | bytes 344072 | tf_op jit(solution)/shard_map/ppermute | solution.py:328
  226.0 5.2 %collective-permute-start.57 = (bf16[16,3584]{1,0:T(8,128)(2,1)S(1)}, bf16[16,3584]{1,0:T(8,128)(2,1)S(1)}, u32[]{:S(2)}, u32[]{:S(2)}) collective-permute-start(bf16[16,3584]{1,0:T(8,128)(2,1)S(1)} %get-tuple-element.220), channel_id=1, source_target_pairs={{0,12},{1,13},{2,14},{3,15},{4,8},{5,9},{6,10},{7,11},{8,20},{9,21... | collective-permute-start | bytes 344072 | tf_op jit(solution)/shard_map/ppermute | solution.py:328
  241.2 3.7 collective-permute-done.49.refs_5_
  250.3 4.2 collective-permute-done.51.refs_2_
  258.6 7.9 %expert_backward_5.1 = (bf16[16,3712]{1,0:T(8,128)(2,1)S(1)}, bf16[16,3712]{1,0:T(8,128)(2,1)S(1)}, bf16[16,3712]{1,0:T(8,128)(2,1)S(1)}, bf16[16,3712]{1,0:T(8,128)(2,1)S(1)}) custom-call(s32[1]{0:T(128)} %bitcast.refs_0_, f32[1,3584]{1,0:T(1,128)S(1)} %copy-done.32, bf16[16,3584]{1,0:T(8,128)(2,1)S(1)} %collective-permute-done.51.refs_2_, ...), custom_call_target="tpu_custom_call" | custom-call | flops 1409286144 | bytes 22020096 | tf_op jit(solution)/shard_map/expert_backward_5/pallas_call | solution.py:455
  266.6 5.0 %collective-permute-start.62 = (bf16[16,3712]{1,0:T(8,128)(2,1)S(1)}, bf16[16,3712]{1,0:T(8,128)(2,1)S(1)}, u32[]{:S(2)}, u32[]{:S(2)}) collective-permute-start(bf16[16,3712]{1,0:T(8,128)(2,1)S(1)} %get-tuple-element.231), channel_id=1, source_target_pairs={{0,6},{1,7},{2,0},{3,1},{4,2},{5,3},{6,4},{7,5},{8,14},{9,15},{10,... | collective-permute-start | bytes 356360 | tf_op jit(solution)/shard_map/ppermute | solution.py:328
  271.6 10.6 %collective-permute-start.69 = (bf16[16,3584]{1,0:T(8,128)(2,1)S(1)}, bf16[16,3584]{1,0:T(8,128)(2,1)S(1)}, u32[]{:S(2)}, u32[]{:S(2)}) collective-permute-start(bf16[16,3584]{1,0:T(8,128)(2,1)S(1)} %get-tuple-element.244), channel_id=1, source_target_pairs={{0,8},{1,9},{2,10},{3,11},{4,12},{5,13},{6,14},{7,15},{8,16},{9,17... | collective-permute-start | bytes 344072 | tf_op jit(solution)/shard_map/ppermute | solution.py:328
  282.2 5.3 %collective-permute-start.70 = (bf16[16,3584]{1,0:T(8,128)(2,1)S(1)}, bf16[16,3584]{1,0:T(8,128)(2,1)S(1)}, u32[]{:S(2)}, u32[]{:S(2)}) collective-permute-start(bf16[16,3584]{1,0:T(8,128)(2,1)S(1)} %get-tuple-element.245), channel_id=1, source_target_pairs={{0,14},{1,15},{2,8},{3,9},{4,10},{5,11},{6,12},{7,13},{8,22},{9,23... | collective-permute-start | bytes 344072 | tf_op jit(solution)/shard_map/ppermute | solution.py:328
  287.5 5.5 %collective-permute-start.71 = (bf16[16,3584]{1,0:T(8,128)(2,1)S(1)}, bf16[16,3584]{1,0:T(8,128)(2,1)S(1)}, u32[]{:S(2)}, u32[]{:S(2)}) collective-permute-start(bf16[16,3584]{1,0:T(8,128)(2,1)S(1)} %get-tuple-element.246), channel_id=1, source_target_pairs={{0,12},{1,13},{2,14},{3,15},{4,8},{5,9},{6,10},{7,11},{8,20},{9,21... | collective-permute-start | bytes 344072 | tf_op jit(solution)/shard_map/ppermute | solution.py:328
  302.1 4.6 collective-permute-done.63.refs_5_
  329.0 11.8 %expert_backward_6.1 = (bf16[16,3712]{1,0:T(8,128)(2,1)S(1)}, bf16[16,3712]{1,0:T(8,128)(2,1)S(1)}, bf16[16,3712]{1,0:T(8,128)(2,1)S(1)}, bf16[16,3712]{1,0:T(8,128)(2,1)S(1)}) custom-call(s32[1]{0:T(128)} %bitcast.refs_0_, f32[1,3584]{1,0:T(1,128)S(1)} %copy-done.32, bf16[16,3584]{1,0:T(8,128)(2,1)S(1)} %copy-done.63, bf16[16,3584]{1,0:T(8,128)(2,1)S(1)} %copy-done.65, ...), custom_call_target="tpu_custom_call" | custom-call | flops 1409286144 | bytes 22020096 | tf_op jit(solution)/shard_map/expert_backward_6/pallas_call | solution.py:455
  340.9 3.6 collective-permute-start.76
  346.8 4.6 collective-permute-done.77.refs_5_
  357.7 6.3 %collective-permute-done.79.refs_2_ = bf16[16,3584]{1,0:T(8,128)(2,1)S(1)} collective-permute-done((bf16[16,3584]{1,0:T(8,128)(2,1)S(1)}, bf16[16,3584]{1,0:T(8,128)(2,1)S(1)}, u32[]{:S(2)}, u32[]{:S(2)}) %collective-permute-start.79) | collective-permute-done | bytes 114720 | tf_op jit(solution)/shard_map/ppermute | solution.py:328
  369.6 12.4 %expert_backward_7.1 = (bf16[16,3712]{1,0:T(8,128)(2,1)S(1)}, bf16[16,3712]{1,0:T(8,128)(2,1)S(1)}, bf16[16,3712]{1,0:T(8,128)(2,1)S(1)}, bf16[16,3712]{1,0:T(8,128)(2,1)S(1)}) custom-call(s32[1]{0:T(128)} %bitcast.refs_0_, f32[1,3584]{1,0:T(1,128)S(1)} %copy-done.32, bf16[16,3584]{1,0:T(8,128)(2,1)S(1)} %collective-permute-done.79.refs_2_, ...), custom_call_target="tpu_custom_call" | custom-call | flops 1409286144 | bytes 22020096 | tf_op jit(solution)/shard_map/expert_backward_7/pallas_call | solution.py:455
  382.0 3.8 collective-permute-start.83
  388.1 4.6 collective-permute-done.84.refs_5_
  398.9 4.8 %collective-permute-done.86.refs_2_ = bf16[16,3584]{1,0:T(8,128)(2,1)S(1)} collective-permute-done((bf16[16,3584]{1,0:T(8,128)(2,1)S(1)}, bf16[16,3584]{1,0:T(8,128)(2,1)S(1)}, u32[]{:S(2)}, u32[]{:S(2)}) %collective-permute-start.86) | collective-permute-done | bytes 114720 | tf_op jit(solution)/shard_map/ppermute | solution.py:328
  410.0 11.8 %expert_backward_8.1 = (bf16[16,3712]{1,0:T(8,128)(2,1)S(1)}, bf16[16,3712]{1,0:T(8,128)(2,1)S(1)}, bf16[16,3712]{1,0:T(8,128)(2,1)S(1)}, bf16[16,3712]{1,0:T(8,128)(2,1)S(1)}) custom-call(s32[1]{0:T(128)} %bitcast.refs_0_, f32[1,3584]{1,0:T(1,128)S(1)} %copy-done.32, bf16[16,3584]{1,0:T(8,128)(2,1)S(1)} %collective-permute-done.86.refs_2_, ...), custom_call_target="tpu_custom_call" | custom-call | flops 1409286144 | bytes 22020096 | tf_op jit(solution)/shard_map/expert_backward_8/pallas_call | solution.py:455
  426.9 4.6 collective-permute-done.91.refs_5_
  437.7 4.6 collective-permute-done.93.refs_2_
  442.3 3.6 collective-permute-done.94.refs_3_
  449.4 11.7 %expert_backward_9.1 = (bf16[16,3712]{1,0:T(8,128)(2,1)S(1)}, bf16[16,3712]{1,0:T(8,128)(2,1)S(1)}, bf16[16,3712]{1,0:T(8,128)(2,1)S(1)}, bf16[16,3712]{1,0:T(8,128)(2,1)S(1)}) custom-call(s32[1]{0:T(128)} %bitcast.refs_0_, f32[1,3584]{1,0:T(1,128)S(1)} %copy-done.32, bf16[16,3584]{1,0:T(8,128)(2,1)S(1)} %collective-permute-done.93.refs_2_, ...), custom_call_target="tpu_custom_call" | custom-call | flops 1409286144 | bytes 22020096 | tf_op jit(solution)/shard_map/expert_backward_9/pallas_call | solution.py:455
  466.0 4.9 %collective-permute-done.98.refs_5_ = bf16[16,3712]{1,0:T(8,128)(2,1)S(1)} collective-permute-done((bf16[16,3712]{1,0:T(8,128)(2,1)S(1)}, bf16[16,3712]{1,0:T(8,128)(2,1)S(1)}, u32[]{:S(2)}, u32[]{:S(2)}) %collective-permute-start.98) | collective-permute-done | bytes 118816 | tf_op jit(solution)/shard_map/ppermute | solution.py:328
  (344 shorter events, 188.0 us)
Async XLA Ops:
  0.6 26.7 %collective-permute-start.7 = (bf16[3584,512]{1,0:T(8,128)(2,1)}, bf16[3584,512]{1,0:T(8,128)(2,1)}, u32[]{:S(2)}, u32[]{:S(2)}) collective-permute-start(bf16[3584,512]{1,0:T(8,128)(2,1)} %bitcast.30), channel_id=1, source_target_pairs={{0,1},{1,0},{2,3},{3,2},{4,5},{5,4},{6,7},{7,6},{8,9},{9,8},{10,11... | collective-permute-start | bytes 11010056 | tf_op jit(solution)/shard_map/ppermute | solution.py:347
  1.1 27.5 %collective-permute-start.8 = (bf16[3584,512]{1,0:T(8,128)(2,1)}, bf16[3584,512]{1,0:T(8,128)(2,1)}, u32[]{:S(2)}, u32[]{:S(2)}) collective-permute-start(bf16[3584,512]{1,0:T(8,128)(2,1)} %bitcast.45), channel_id=1, source_target_pairs={{0,1},{1,0},{2,3},{3,2},{4,5},{5,4},{6,7},{7,6},{8,9},{9,8},{10,11... | collective-permute-start | bytes 11010056 | tf_op jit(solution)/shard_map/ppermute | solution.py:347
  1.2 27.4 %collective-permute-start.9 = (bf16[512,3584]{1,0:T(8,128)(2,1)}, bf16[512,3584]{1,0:T(8,128)(2,1)}, u32[]{:S(2)}, u32[]{:S(2)}) collective-permute-start(bf16[512,3584]{1,0:T(8,128)(2,1)} %bitcast.60), channel_id=1, source_target_pairs={{0,1},{1,0},{2,3},{3,2},{4,5},{5,4},{6,7},{7,6},{8,9},{9,8},{10,11... | collective-permute-start | bytes 11010056 | tf_op jit(solution)/shard_map/ppermute | solution.py:347
  13.1 10.8 %collective-permute-start.11 = (bf16[16,3712]{1,0:T(8,128)(2,1)S(1)}, bf16[16,3712]{1,0:T(8,128)(2,1)S(1)}, u32[]{:S(2)}, u32[]{:S(2)}) collective-permute-start(bf16[16,3712]{1,0:T(8,128)(2,1)S(1)} %get-tuple-element.150), channel_id=1, source_target_pairs={{0,4},{1,5},{2,6},{3,7},{4,0},{5,1},{6,2},{7,3},{8,12},{9,13},{10,... | collective-permute-start | bytes 356360 | tf_op jit(solution)/shard_map/ppermute | solution.py:328
  23.9 23.2 %collective-permute-start.1 = (bf16[32,3584]{1,0:T(8,128)(2,1)S(1)}, bf16[32,3584]{1,0:T(8,128)(2,1)S(1)}, u32[]{:S(2)}, u32[]{:S(2)}) collective-permute-start(bf16[32,3584]{1,0:T(8,128)(2,1)S(1)} %get-tuple-element.302), channel_id=1, source_target_pairs={{8,0},{0,24},{9,1},{1,25},{10,2},{2,26},{11,3},{3,27},{12,4},{4,28... | collective-permute-start | bytes 688136 | tf_op jit(solution)/shard_map/ppermute | solution.py:375
  26.1 22.5 %collective-permute-start.2 = (bf16[32,3584]{1,0:T(8,128)(2,1)S(1)}, bf16[32,3584]{1,0:T(8,128)(2,1)S(1)}, u32[]{:S(2)}, u32[]{:S(2)}) collective-permute-start(bf16[32,3584]{1,0:T(8,128)(2,1)S(1)} %get-tuple-element.303), channel_id=1, source_target_pairs={{16,0},{8,24},{17,1},{9,25},{18,2},{10,26},{19,3},{11,27},{20,4},{... | collective-permute-start | bytes 688136 | tf_op jit(solution)/shard_map/ppermute | solution.py:375
  27.4 25.0 %collective-permute-start.3 = (bf16[32,3584]{1,0:T(8,128)(2,1)S(1)}, bf16[32,3584]{1,0:T(8,128)(2,1)S(1)}, u32[]{:S(2)}, u32[]{:S(2)}) collective-permute-start(bf16[32,3584]{1,0:T(8,128)(2,1)S(1)} %get-tuple-element.304), channel_id=1, source_target_pairs={{24,0},{16,24},{25,1},{17,25},{26,2},{18,26},{27,3},{19,27},{28,4}... | collective-permute-start | bytes 688136 | tf_op jit(solution)/shard_map/ppermute | solution.py:375
  42.0 11.1 %collective-permute-start.13 = (bf16[16,3584]{1,0:T(8,128)(2,1)S(1)}, bf16[16,3584]{1,0:T(8,128)(2,1)S(1)}, u32[]{:S(2)}, u32[]{:S(2)}) collective-permute-start(bf16[16,3584]{1,0:T(8,128)(2,1)S(1)} %get-tuple-element.152), channel_id=1, source_target_pairs={{0,8},{1,9},{2,10},{3,11},{4,12},{5,13},{6,14},{7,15},{8,16},{9,17... | collective-permute-start | bytes 344072 | tf_op jit(solution)/shard_map/ppermute | solution.py:328
  61.1 41.1 %collective-permute-start.6 = (bf16[4,16,3584]{2,1,0:T(8,128)(2,1)S(1)}, bf16[4,16,3584]{2,1,0:T(8,128)(2,1)S(1)}, u32[]{:S(2)}, u32[]{:S(2)}) collective-permute-start(bf16[4,16,3584]{2,1,0:T(8,128)(2,1)S(1)} %get-tuple-element.299), channel_id=1, source_target_pairs={{24,30},{25,31},{26,24},{27,25},{28,26},{29,27},{30,28},{31,29}} | collective-permute-start | bytes 1376264 | tf_op jit(solution)/shard_map/ppermute | solution.py:328
  73.1 22.3 %collective-permute-start.20 = (bf16[16,3584]{1,0:T(8,128)(2,1)S(1)}, bf16[16,3584]{1,0:T(8,128)(2,1)S(1)}, u32[]{:S(2)}, u32[]{:S(2)}) collective-permute-start(bf16[16,3584]{1,0:T(8,128)(2,1)S(1)} %get-tuple-element.160), channel_id=1, source_target_pairs={{0,8},{1,9},{2,10},{3,11},{4,12},{5,13},{6,14},{7,15},{8,16},{9,17... | collective-permute-start | bytes 344072 | tf_op jit(solution)/shard_map/ppermute | solution.py:328
  78.1 17.9 %collective-permute-start.21 = (bf16[16,3584]{1,0:T(8,128)(2,1)S(1)}, bf16[16,3584]{1,0:T(8,128)(2,1)S(1)}, u32[]{:S(2)}, u32[]{:S(2)}) collective-permute-start(bf16[16,3584]{1,0:T(8,128)(2,1)S(1)} %get-tuple-element.161), channel_id=1, source_target_pairs={{0,14},{1,15},{2,8},{3,9},{4,10},{5,11},{6,12},{7,13},{8,22},{9,23... | collective-permute-start | bytes 344072 | tf_op jit(solution)/shard_map/ppermute | solution.py:328
  82.0 14.8 %collective-permute-start.22 = (bf16[16,3584]{1,0:T(8,128)(2,1)S(1)}, bf16[16,3584]{1,0:T(8,128)(2,1)S(1)}, u32[]{:S(2)}, u32[]{:S(2)}) collective-permute-start(bf16[16,3584]{1,0:T(8,128)(2,1)S(1)} %get-tuple-element.162), channel_id=1, source_target_pairs={{0,12},{1,13},{2,14},{3,15},{4,8},{5,9},{6,10},{7,11},{8,20},{9,21... | collective-permute-start | bytes 344072 | tf_op jit(solution)/shard_map/ppermute | solution.py:328
  95.4 36.6 %collective-permute-start.5 = (bf16[4,16,3584]{2,1,0:T(8,128)(2,1)S(1)}, bf16[4,16,3584]{2,1,0:T(8,128)(2,1)S(1)}, u32[]{:S(2)}, u32[]{:S(2)}) collective-permute-start(bf16[4,16,3584]{2,1,0:T(8,128)(2,1)S(1)} %get-tuple-element.300), channel_id=1, source_target_pairs={{24,28},{25,29},{26,30},{27,31},{28,24},{29,25},{30,26},{31,27}} | collective-permute-start | bytes 1376264 | tf_op jit(solution)/shard_map/ppermute | solution.py:328
  96.1 48.9 %collective-permute-start.4 = (bf16[4,16,3584]{2,1,0:T(8,128)(2,1)S(1)}, bf16[4,16,3584]{2,1,0:T(8,128)(2,1)S(1)}, u32[]{:S(2)}, u32[]{:S(2)}) collective-permute-start(bf16[4,16,3584]{2,1,0:T(8,128)(2,1)S(1)} %get-tuple-element.301), channel_id=1, source_target_pairs={{24,26},{25,27},{26,28},{27,29},{28,30},{29,31},{30,24},{31,25}} | collective-permute-start | bytes 1376264 | tf_op jit(solution)/shard_map/ppermute | solution.py:328
  114.6 20.5 %collective-permute-start.27 = (bf16[16,3584]{1,0:T(8,128)(2,1)S(1)}, bf16[16,3584]{1,0:T(8,128)(2,1)S(1)}, u32[]{:S(2)}, u32[]{:S(2)}) collective-permute-start(bf16[16,3584]{1,0:T(8,128)(2,1)S(1)} %get-tuple-element.168), channel_id=1, source_target_pairs={{0,8},{1,9},{2,10},{3,11},{4,12},{5,13},{6,14},{7,15},{8,16},{9,17... | collective-permute-start | bytes 344072 | tf_op jit(solution)/shard_map/ppermute | solution.py:328
  120.6 14.5 %collective-permute-start.28 = (bf16[16,3584]{1,0:T(8,128)(2,1)S(1)}, bf16[16,3584]{1,0:T(8,128)(2,1)S(1)}, u32[]{:S(2)}, u32[]{:S(2)}) collective-permute-start(bf16[16,3584]{1,0:T(8,128)(2,1)S(1)} %get-tuple-element.169), channel_id=1, source_target_pairs={{0,14},{1,15},{2,8},{3,9},{4,10},{5,11},{6,12},{7,13},{8,22},{9,23... | collective-permute-start | bytes 344072 | tf_op jit(solution)/shard_map/ppermute | solution.py:328
  155.3 16.6 %collective-permute-start.41 = (bf16[16,3584]{1,0:T(8,128)(2,1)S(1)}, bf16[16,3584]{1,0:T(8,128)(2,1)S(1)}, u32[]{:S(2)}, u32[]{:S(2)}) collective-permute-start(bf16[16,3584]{1,0:T(8,128)(2,1)S(1)} %get-tuple-element.192), channel_id=1, source_target_pairs={{0,8},{1,9},{2,10},{3,11},{4,12},{5,13},{6,14},{7,15},{8,16},{9,17... | collective-permute-start | bytes 344072 | tf_op jit(solution)/shard_map/ppermute | solution.py:328
  160.5 11.4 %collective-permute-start.42 = (bf16[16,3584]{1,0:T(8,128)(2,1)S(1)}, bf16[16,3584]{1,0:T(8,128)(2,1)S(1)}, u32[]{:S(2)}, u32[]{:S(2)}) collective-permute-start(bf16[16,3584]{1,0:T(8,128)(2,1)S(1)} %get-tuple-element.193), channel_id=1, source_target_pairs={{0,14},{1,15},{2,8},{3,9},{4,10},{5,11},{6,12},{7,13},{8,22},{9,23... | collective-permute-start | bytes 344072 | tf_op jit(solution)/shard_map/ppermute | solution.py:328
  168.4 13.7 %collective-permute-start.34 = (bf16[16,3712]{1,0:T(8,128)(2,1)S(1)}, bf16[16,3712]{1,0:T(8,128)(2,1)S(1)}, u32[]{:S(2)}, u32[]{:S(2)}) collective-permute-start(bf16[16,3712]{1,0:T(8,128)(2,1)S(1)} %get-tuple-element.181), channel_id=1, source_target_pairs={{0,6},{1,7},{2,0},{3,1},{4,2},{5,3},{6,4},{7,5},{8,14},{9,15},{10,... | collective-permute-start | bytes 356360 | tf_op jit(solution)/shard_map/ppermute | solution.py:328
  171.8 14.4 %collective-permute-start.35 = (bf16[16,3712]{1,0:T(8,128)(2,1)S(1)}, bf16[16,3712]{1,0:T(8,128)(2,1)S(1)}, u32[]{:S(2)}, u32[]{:S(2)}) collective-permute-start(bf16[16,3712]{1,0:T(8,128)(2,1)S(1)} %get-tuple-element.182), channel_id=1, source_target_pairs={{0,4},{1,5},{2,6},{3,7},{4,0},{5,1},{6,2},{7,3},{8,12},{9,13},{10,... | collective-permute-start | bytes 356360 | tf_op jit(solution)/shard_map/ppermute | solution.py:328
  171.9 14.3 %collective-permute-start.36 = (bf16[16,3712]{1,0:T(8,128)(2,1)S(1)}, bf16[16,3712]{1,0:T(8,128)(2,1)S(1)}, u32[]{:S(2)}, u32[]{:S(2)}) collective-permute-start(bf16[16,3712]{1,0:T(8,128)(2,1)S(1)} %get-tuple-element.183), channel_id=1, source_target_pairs={{0,2},{1,3},{2,4},{3,5},{4,6},{5,7},{6,0},{7,1},{8,10},{9,11},{10,... | collective-permute-start | bytes 356360 | tf_op jit(solution)/shard_map/ppermute | solution.py:328
  173.4 15.8 %collective-permute-start.45 = (bf16[16,3712]{1,0:T(8,128)(2,1)S(1)}, bf16[16,3712]{1,0:T(8,128)(2,1)S(1)}, u32[]{:S(2)}, u32[]{:S(2)}) collective-permute-start(bf16[16,3712]{1,0:T(8,128)(2,1)S(1)} %get-tuple-element.197), channel_id=1, source_target_pairs={{0,2},{1,3},{2,4},{3,5},{4,6},{5,7},{6,0},{7,1},{8,10},{9,11},{10,... | collective-permute-start | bytes 356360 | tf_op jit(solution)/shard_map/ppermute | solution.py:328
  189.2 11.1 %collective-permute-start.39 = (bf16[16,3584]{1,0:T(8,128)(2,1)S(1)}, bf16[16,3584]{1,0:T(8,128)(2,1)S(1)}, u32[]{:S(2)}, u32[]{:S(2)}) collective-permute-start(bf16[16,3584]{1,0:T(8,128)(2,1)S(1)} %get-tuple-element.186), channel_id=1, source_target_pairs={{8,4},{9,5},{10,6},{11,7},{12,0},{13,1},{14,2},{15,3},{16,12},{17,... | collective-permute-start | bytes 344072 | tf_op jit(solution)/shard_map/ppermute | solution.py:328
  190.5 10.7 %collective-permute-start.40 = (bf16[16,3584]{1,0:T(8,128)(2,1)S(1)}, bf16[16,3584]{1,0:T(8,128)(2,1)S(1)}, u32[]{:S(2)}, u32[]{:S(2)}) collective-permute-start(bf16[16,3584]{1,0:T(8,128)(2,1)S(1)} %get-tuple-element.187), channel_id=1, source_target_pairs={{8,6},{9,7},{10,0},{11,1},{12,2},{13,3},{14,4},{15,5},{16,14},{17,... | collective-permute-start | bytes 344072 | tf_op jit(solution)/shard_map/ppermute | solution.py:328
  201.4 37.6 %collective-permute-start.48 = (bf16[16,3712]{1,0:T(8,128)(2,1)S(1)}, bf16[16,3712]{1,0:T(8,128)(2,1)S(1)}, u32[]{:S(2)}, u32[]{:S(2)}) collective-permute-start(bf16[16,3712]{1,0:T(8,128)(2,1)S(1)} %get-tuple-element.205), channel_id=1, source_target_pairs={{0,6},{1,7},{2,0},{3,1},{4,2},{5,3},{6,4},{7,5},{8,14},{9,15},{10,... | collective-permute-start | bytes 356360 | tf_op jit(solution)/shard_map/ppermute | solution.py:328
  203.7 28.8 %collective-permute-start.55 = (bf16[16,3584]{1,0:T(8,128)(2,1)S(1)}, bf16[16,3584]{1,0:T(8,128)(2,1)S(1)}, u32[]{:S(2)}, u32[]{:S(2)}) collective-permute-start(bf16[16,3584]{1,0:T(8,128)(2,1)S(1)} %get-tuple-element.218), channel_id=1, source_target_pairs={{0,8},{1,9},{2,10},{3,11},{4,12},{5,13},{6,14},{7,15},{8,16},{9,17... | collective-permute-start | bytes 344072 | tf_op jit(solution)/shard_map/ppermute | solution.py:328
  209.4 25.2 %collective-permute-start.56 = (bf16[16,3584]{1,0:T(8,128)(2,1)S(1)}, bf16[16,3584]{1,0:T(8,128)(2,1)S(1)}, u32[]{:S(2)}, u32[]{:S(2)}) collective-permute-start(bf16[16,3584]{1,0:T(8,128)(2,1)S(1)} %get-tuple-element.219), channel_id=1, source_target_pairs={{0,14},{1,15},{2,8},{3,9},{4,10},{5,11},{6,12},{7,13},{8,22},{9,23... | collective-permute-start | bytes 344072 | tf_op jit(solution)/shard_map/ppermute | solution.py:328
  232.5 12.5 %collective-permute-start.49 = (bf16[16,3712]{1,0:T(8,128)(2,1)S(1)}, bf16[16,3712]{1,0:T(8,128)(2,1)S(1)}, u32[]{:S(2)}, u32[]{:S(2)}) collective-permute-start(bf16[16,3712]{1,0:T(8,128)(2,1)S(1)} %get-tuple-element.206), channel_id=1, source_target_pairs={{0,4},{1,5},{2,6},{3,7},{4,0},{5,1},{6,2},{7,3},{8,12},{9,13},{10,... | collective-permute-start | bytes 356360 | tf_op jit(solution)/shard_map/ppermute | solution.py:328
  236.3 11.2 %collective-permute-start.59 = (bf16[16,3712]{1,0:T(8,128)(2,1)S(1)}, bf16[16,3712]{1,0:T(8,128)(2,1)S(1)}, u32[]{:S(2)}, u32[]{:S(2)}) collective-permute-start(bf16[16,3712]{1,0:T(8,128)(2,1)S(1)} %get-tuple-element.223), channel_id=1, source_target_pairs={{0,2},{1,3},{2,4},{3,5},{4,6},{5,7},{6,0},{7,1},{8,10},{9,11},{10,... | collective-permute-start | bytes 356360 | tf_op jit(solution)/shard_map/ppermute | solution.py:328
  239.0 11.2 %collective-permute-start.61 = (bf16[16,3712]{1,0:T(8,128)(2,1)S(1)}, bf16[16,3712]{1,0:T(8,128)(2,1)S(1)}, u32[]{:S(2)}, u32[]{:S(2)}) collective-permute-start(bf16[16,3712]{1,0:T(8,128)(2,1)S(1)} %get-tuple-element.225), channel_id=1, source_target_pairs={{0,6},{1,7},{2,0},{3,1},{4,2},{5,3},{6,4},{7,5},{8,14},{9,15},{10,... | collective-permute-start | bytes 356360 | tf_op jit(solution)/shard_map/ppermute | solution.py:328
  247.6 11.0 %collective-permute-start.53 = (bf16[16,3584]{1,0:T(8,128)(2,1)S(1)}, bf16[16,3584]{1,0:T(8,128)(2,1)S(1)}, u32[]{:S(2)}, u32[]{:S(2)}) collective-permute-start(bf16[16,3584]{1,0:T(8,128)(2,1)S(1)} %get-tuple-element.212), channel_id=1, source_target_pairs={{8,4},{9,5},{10,6},{11,7},{12,0},{13,1},{14,2},{15,3},{16,12},{17,... | collective-permute-start | bytes 344072 | tf_op jit(solution)/shard_map/ppermute | solution.py:328
  266.6 34.3 %collective-permute-start.62 = (bf16[16,3712]{1,0:T(8,128)(2,1)S(1)}, bf16[16,3712]{1,0:T(8,128)(2,1)S(1)}, u32[]{:S(2)}, u32[]{:S(2)}) collective-permute-start(bf16[16,3712]{1,0:T(8,128)(2,1)S(1)} %get-tuple-element.231), channel_id=1, source_target_pairs={{0,6},{1,7},{2,0},{3,1},{4,2},{5,3},{6,4},{7,5},{8,14},{9,15},{10,... | collective-permute-start | bytes 356360 | tf_op jit(solution)/shard_map/ppermute | solution.py:328
  271.6 23.1 %collective-permute-start.69 = (bf16[16,3584]{1,0:T(8,128)(2,1)S(1)}, bf16[16,3584]{1,0:T(8,128)(2,1)S(1)}, u32[]{:S(2)}, u32[]{:S(2)}) collective-permute-start(bf16[16,3584]{1,0:T(8,128)(2,1)S(1)} %get-tuple-element.244), channel_id=1, source_target_pairs={{0,8},{1,9},{2,10},{3,11},{4,12},{5,13},{6,14},{7,15},{8,16},{9,17... | collective-permute-start | bytes 344072 | tf_op jit(solution)/shard_map/ppermute | solution.py:328
  282.2 14.3 %collective-permute-start.70 = (bf16[16,3584]{1,0:T(8,128)(2,1)S(1)}, bf16[16,3584]{1,0:T(8,128)(2,1)S(1)}, u32[]{:S(2)}, u32[]{:S(2)}) collective-permute-start(bf16[16,3584]{1,0:T(8,128)(2,1)S(1)} %get-tuple-element.245), channel_id=1, source_target_pairs={{0,14},{1,15},{2,8},{3,9},{4,10},{5,11},{6,12},{7,13},{8,22},{9,23... | collective-permute-start | bytes 344072 | tf_op jit(solution)/shard_map/ppermute | solution.py:328
  294.7 12.0 %collective-permute-start.63 = (bf16[16,3712]{1,0:T(8,128)(2,1)S(1)}, bf16[16,3712]{1,0:T(8,128)(2,1)S(1)}, u32[]{:S(2)}, u32[]{:S(2)}) collective-permute-start(bf16[16,3712]{1,0:T(8,128)(2,1)S(1)} %get-tuple-element.232), channel_id=1, source_target_pairs={{0,4},{1,5},{2,6},{3,7},{4,0},{5,1},{6,2},{7,3},{8,12},{9,13},{10,... | collective-permute-start | bytes 356360 | tf_op jit(solution)/shard_map/ppermute | solution.py:328
  298.3 11.1 %collective-permute-start.73 = (bf16[16,3712]{1,0:T(8,128)(2,1)S(1)}, bf16[16,3712]{1,0:T(8,128)(2,1)S(1)}, u32[]{:S(2)}, u32[]{:S(2)}) collective-permute-start(bf16[16,3712]{1,0:T(8,128)(2,1)S(1)} %get-tuple-element.249), channel_id=1, source_target_pairs={{0,2},{1,3},{2,4},{3,5},{4,6},{5,7},{6,0},{7,1},{8,10},{9,11},{10,... | collective-permute-start | bytes 356360 | tf_op jit(solution)/shard_map/ppermute | solution.py:328
  298.5 12.2 %collective-permute-start.74 = (bf16[16,3712]{1,0:T(8,128)(2,1)S(1)}, bf16[16,3712]{1,0:T(8,128)(2,1)S(1)}, u32[]{:S(2)}, u32[]{:S(2)}) collective-permute-start(bf16[16,3712]{1,0:T(8,128)(2,1)S(1)} %get-tuple-element.250), channel_id=1, source_target_pairs={{0,4},{1,5},{2,6},{3,7},{4,0},{5,1},{6,2},{7,3},{8,12},{9,13},{10,... | collective-permute-start | bytes 356360 | tf_op jit(solution)/shard_map/ppermute | solution.py:328
  300.9 11.1 %collective-permute-start.75 = (bf16[16,3712]{1,0:T(8,128)(2,1)S(1)}, bf16[16,3712]{1,0:T(8,128)(2,1)S(1)}, u32[]{:S(2)}, u32[]{:S(2)}) collective-permute-start(bf16[16,3712]{1,0:T(8,128)(2,1)S(1)} %get-tuple-element.251), channel_id=1, source_target_pairs={{0,6},{1,7},{2,0},{3,1},{4,2},{5,3},{6,4},{7,5},{8,14},{9,15},{10,... | collective-permute-start | bytes 356360 | tf_op jit(solution)/shard_map/ppermute | solution.py:328
  352.4 11.7 %collective-permute-start.79 = (bf16[16,3584]{1,0:T(8,128)(2,1)S(1)}, bf16[16,3584]{1,0:T(8,128)(2,1)S(1)}, u32[]{:S(2)}, u32[]{:S(2)}) collective-permute-start(bf16[16,3584]{1,0:T(8,128)(2,1)S(1)} %get-tuple-element.262), channel_id=1, source_target_pairs={{8,0},{9,1},{10,2},{11,3},{12,4},{13,5},{14,6},{15,7},{16,8},{17,9... | collective-permute-start | bytes 344072 | tf_op jit(solution)/shard_map/ppermute | solution.py:328
  353.7 11.9 %collective-permute-start.80 = (bf16[16,3584]{1,0:T(8,128)(2,1)S(1)}, bf16[16,3584]{1,0:T(8,128)(2,1)S(1)}, u32[]{:S(2)}, u32[]{:S(2)}) collective-permute-start(bf16[16,3584]{1,0:T(8,128)(2,1)S(1)} %get-tuple-element.263), channel_id=1, source_target_pairs={{8,2},{9,3},{10,4},{11,5},{12,6},{13,7},{14,0},{15,1},{16,10},{17,... | collective-permute-start | bytes 344072 | tf_op jit(solution)/shard_map/ppermute | solution.py:328
  355.0 13.8 %collective-permute-start.81 = (bf16[16,3584]{1,0:T(8,128)(2,1)S(1)}, bf16[16,3584]{1,0:T(8,128)(2,1)S(1)}, u32[]{:S(2)}, u32[]{:S(2)}) collective-permute-start(bf16[16,3584]{1,0:T(8,128)(2,1)S(1)} %get-tuple-element.264), channel_id=1, source_target_pairs={{8,4},{9,5},{10,6},{11,7},{12,0},{13,1},{14,2},{15,3},{16,12},{17,... | collective-permute-start | bytes 344072 | tf_op jit(solution)/shard_map/ppermute | solution.py:328
  356.3 13.2 %collective-permute-start.82 = (bf16[16,3584]{1,0:T(8,128)(2,1)S(1)}, bf16[16,3584]{1,0:T(8,128)(2,1)S(1)}, u32[]{:S(2)}, u32[]{:S(2)}) collective-permute-start(bf16[16,3584]{1,0:T(8,128)(2,1)S(1)} %get-tuple-element.265), channel_id=1, source_target_pairs={{8,6},{9,7},{10,0},{11,1},{12,2},{13,3},{14,4},{15,5},{16,14},{17,... | collective-permute-start | bytes 344072 | tf_op jit(solution)/shard_map/ppermute | solution.py:328
  395.0 11.5 %collective-permute-start.87 = (bf16[16,3584]{1,0:T(8,128)(2,1)S(1)}, bf16[16,3584]{1,0:T(8,128)(2,1)S(1)}, u32[]{:S(2)}, u32[]{:S(2)}) collective-permute-start(bf16[16,3584]{1,0:T(8,128)(2,1)S(1)} %get-tuple-element.273), channel_id=1, source_target_pairs={{8,2},{9,3},{10,4},{11,5},{12,6},{13,7},{14,0},{15,1},{16,10},{17,... | collective-permute-start | bytes 344072 | tf_op jit(solution)/shard_map/ppermute | solution.py:328
  396.3 13.4 %collective-permute-start.88 = (bf16[16,3584]{1,0:T(8,128)(2,1)S(1)}, bf16[16,3584]{1,0:T(8,128)(2,1)S(1)}, u32[]{:S(2)}, u32[]{:S(2)}) collective-permute-start(bf16[16,3584]{1,0:T(8,128)(2,1)S(1)} %get-tuple-element.274), channel_id=1, source_target_pairs={{8,4},{9,5},{10,6},{11,7},{12,0},{13,1},{14,2},{15,3},{16,12},{17,... | collective-permute-start | bytes 344072 | tf_op jit(solution)/shard_map/ppermute | solution.py:328
  397.6 12.4 %collective-permute-start.89 = (bf16[16,3584]{1,0:T(8,128)(2,1)S(1)}, bf16[16,3584]{1,0:T(8,128)(2,1)S(1)}, u32[]{:S(2)}, u32[]{:S(2)}) collective-permute-start(bf16[16,3584]{1,0:T(8,128)(2,1)S(1)} %get-tuple-element.275), channel_id=1, source_target_pairs={{8,6},{9,7},{10,0},{11,1},{12,2},{13,3},{14,4},{15,5},{16,14},{17,... | collective-permute-start | bytes 344072 | tf_op jit(solution)/shard_map/ppermute | solution.py:328
  433.8 12.1 %collective-permute-start.94 = (bf16[16,3584]{1,0:T(8,128)(2,1)S(1)}, bf16[16,3584]{1,0:T(8,128)(2,1)S(1)}, u32[]{:S(2)}, u32[]{:S(2)}) collective-permute-start(bf16[16,3584]{1,0:T(8,128)(2,1)S(1)} %get-tuple-element.283), channel_id=1, source_target_pairs={{8,2},{9,3},{10,4},{11,5},{12,6},{13,7},{14,0},{15,1},{16,10},{17,... | collective-permute-start | bytes 344072 | tf_op jit(solution)/shard_map/ppermute | solution.py:328
  435.1 14.0 %collective-permute-start.95 = (bf16[16,3584]{1,0:T(8,128)(2,1)S(1)}, bf16[16,3584]{1,0:T(8,128)(2,1)S(1)}, u32[]{:S(2)}, u32[]{:S(2)}) collective-permute-start(bf16[16,3584]{1,0:T(8,128)(2,1)S(1)} %get-tuple-element.284), channel_id=1, source_target_pairs={{8,4},{9,5},{10,6},{11,7},{12,0},{13,1},{14,2},{15,3},{16,12},{17,... | collective-permute-start | bytes 344072 | tf_op jit(solution)/shard_map/ppermute | solution.py:328
  436.4 13.0 %collective-permute-start.96 = (bf16[16,3584]{1,0:T(8,128)(2,1)S(1)}, bf16[16,3584]{1,0:T(8,128)(2,1)S(1)}, u32[]{:S(2)}, u32[]{:S(2)}) collective-permute-start(bf16[16,3584]{1,0:T(8,128)(2,1)S(1)} %get-tuple-element.285), channel_id=1, source_target_pairs={{8,6},{9,7},{10,0},{11,1},{12,2},{13,3},{14,4},{15,5},{16,14},{17,... | collective-permute-start | bytes 344072 | tf_op jit(solution)/shard_map/ppermute | solution.py:328
  (123 other events, 2666.6 us)
